TPU v7x, 256 devices: a whole 4x4x8 slice. The times are simulated.
256 devices in a mesh: dp: 4 (over x), seq: 64 (over z, y, core).
Axes of the slice: x: 4, y: 4, z: 8, core: 2. Of those that a mesh axis runs over, the one named last changes fastest.
Arguments:
- hidden_states: bfloat16 [32768, 4096], P(('dp', 'seq')), may hold values from -32 to 32
- q_grads: bfloat16 [32768, 4096], P(('dp', 'seq')), may hold values from -48 to 48
- doc_units: int32 [4, 3], P('dp'), may hold values from 1 to 48, 64 in all within a row
Outputs:
- doc_ratio: float32 [4, 3], P('dp')
- clipped_grad: float32 [64, 512, 512], P('seq', 'dp')
Inputs may be any that keep to these rules, and one draw needn't show every extreme that they name: `doc_units`: each row lists, in order, the lengths of the documents packed into one group's 8192 tokens; a row sums to 64, and each row holds 48 somewhere.
All inputs are finite; a program needn't handle non-finite values.
Results may differ from a plain program's by a relative error of at most 0.00038.
Values may be sent and summed in bfloat16 or wider, within the bound.
No kernel may reach another device: no remote copies, remote signals or barrier semaphores. Data moves between devices by JAX's collectives and lax.ppermute only.
A program may use at most 128 MiB of HBM per device.

v0:
```python
import jax
import jax.numpy as jnp
from jax import lax
from jax.sharding import PartitionSpec as P

UNIT = 128
COL_TILES = 8


def doc_lookup(positions, doc_ends):
    return jnp.sum((doc_ends[None, :] <= positions[:, None]).astype(jnp.int32), axis=1)


def one_hot_docs(doc_ids, doc_count):
    return (doc_ids[:, None] == jnp.arange(doc_count, dtype=jnp.int32)[None, :]).astype(jnp.float32)


def clip_factors(partial_value):
    totals = lax.psum(partial_value, "seq")
    doc_norm = jnp.sqrt(totals)
    threshold = jnp.mean(doc_norm)
    return (doc_norm / threshold, 1.0 / jnp.maximum(doc_norm, threshold))


def masked_terms(flat_acts, flat_grads, pack_doc, doc_count):

    def doc_square(doc_index):
        inside = pack_doc == doc_index
        doc_grads = jnp.where(inside[:, None], flat_grads, jnp.zeros_like(flat_grads))
        product = lax.dot_general(
            flat_acts, doc_grads, (((0,), (0,)), ((), ())), preferred_element_type=jnp.float32
        )
        return jnp.sum(product * product)

    return lax.map(doc_square, jnp.arange(doc_count, dtype=jnp.int32))


def unit_terms(flat_acts, flat_grads, pack_doc, doc_starts, doc_lengths, doc_span, doc_count):
    pack_rows = flat_acts.shape[0]
    rest_span = pack_rows - doc_span
    is_longest = doc_lengths == doc_span
    long_start = jnp.sum(jnp.where(is_longest, doc_starts, 0))
    long_acts = lax.dynamic_slice_in_dim(flat_acts, long_start, doc_span, 0)
    long_grads = lax.dynamic_slice_in_dim(flat_grads, long_start, doc_span, 0)
    long_product = lax.dot_general(
        long_acts, long_grads, (((0,), (0,)), ((), ())), preferred_element_type=jnp.float32
    )
    long_square = jnp.sum(long_product * long_product)
    rest_start = (long_start + doc_span) % pack_rows
    rest_acts = lax.dynamic_slice_in_dim(
        jnp.concatenate([flat_acts, flat_acts], axis=0), rest_start, rest_span, 0
    )
    rest_grads = lax.dynamic_slice_in_dim(
        jnp.concatenate([flat_grads, flat_grads], axis=0), rest_start, rest_span, 0
    )
    rest_doc = lax.dynamic_slice_in_dim(
        jnp.concatenate([pack_doc, pack_doc], axis=0), rest_start, rest_span, 0
    )
    rest_squares = masked_terms(rest_acts, rest_grads, rest_doc, doc_count)
    return jnp.where(is_longest, long_square, rest_squares)


def body(hidden_states, q_grads, doc_units):
    tok_rows, width = hidden_states.shape
    seq_count = lax.axis_size("seq")
    dp_count = lax.axis_size("dp")
    row_tiles = seq_count // COL_TILES
    tile_rows = width // row_tiles
    tile_cols = width // COL_TILES
    pack_rows = tok_rows * seq_count
    doc_span = 3 * pack_rows // 4
    doc_count = doc_units.shape[1]
    doc_lengths = doc_units[0] * UNIT
    doc_ends = jnp.cumsum(doc_lengths)
    doc_starts = doc_ends - doc_lengths
    act_pieces = hidden_states.reshape(tok_rows, row_tiles, tile_rows).transpose(1, 0, 2)
    act_pieces = jnp.broadcast_to(act_pieces[:, None], (row_tiles, COL_TILES, tok_rows, tile_rows))
    act_pieces = act_pieces.reshape(seq_count, tok_rows, tile_rows)
    grad_pieces = q_grads.reshape(tok_rows, COL_TILES, tile_cols).transpose(1, 0, 2)
    grad_pieces = jnp.broadcast_to(grad_pieces[None], (row_tiles, COL_TILES, tok_rows, tile_cols))
    grad_pieces = grad_pieces.reshape(seq_count, tok_rows, tile_cols)
    act_cols, grad_cols = (
        lax.all_to_all(act_pieces, "seq", split_axis=0, concat_axis=0, tiled=True),
        lax.all_to_all(grad_pieces, "seq", split_axis=0, concat_axis=0, tiled=True),
    )
    flat_acts = act_cols.reshape(pack_rows, tile_rows)
    flat_grads = grad_cols.reshape(pack_rows, tile_cols)
    pack_doc = doc_lookup(jnp.arange(pack_rows, dtype=jnp.int32), doc_ends)
    partial_value = unit_terms(
        flat_acts, flat_grads, pack_doc, doc_starts, doc_lengths, doc_span, doc_count
    )
    doc_ratio, clip_factor = clip_factors(partial_value)
    pack_hot = one_hot_docs(pack_doc, doc_count)
    pack_clip = jnp.dot(pack_hot, clip_factor, precision=lax.Precision.HIGHEST)
    scaled_grads = (pack_clip[:, None] * flat_grads.astype(jnp.float32)).astype(jnp.bfloat16)
    share_rows = tile_rows // dp_count
    whole_tile = lax.psum(
        lax.dot_general(
            flat_acts, scaled_grads, (((0,), (0,)), ((), ())), preferred_element_type=jnp.float32
        ),
        "dp",
    )
    share = lax.dynamic_slice_in_dim(whole_tile, lax.axis_index("dp") * share_rows, share_rows, 0)
    clipped = share * (width / (dp_count * doc_count))
    return (doc_ratio[None, :], clipped[None])


def solution(mesh):
    in_specs = (P(("dp", "seq"), None), P(("dp", "seq"), None), P("dp", None))
    out_specs = (P("dp", None), P("seq", "dp", None))
    return jax.shard_map(body, mesh=mesh, in_specs=in_specs, out_specs=out_specs, check_vma=False)
```

profile of v0, /device:TPU:1, one launch (start us, length us, event | category | flops | bytes accessed | tf_op | source)
XLA Modules:
  0.0 641.6 jit_solution(9377255834667953196)
XLA Ops:
  7.2 1.6 copy.17
  9.1 4.2 broadcast_in_dim.44
  13.3 13.5 %all-to-all-start = ((bf16[64,128,512]{2,1,0:T(8,128)(2,1)}), bf16[64,128,512]{2,1,0:T(8,128)(2,1)}, u32[]{:S(2)}, u32[]{:S(2)}) async-start(bf16[64,128,512]{2,1,0:T(8,128)(2,1)} %bitcast.47), calls=%async_computation | async-start | bytes 16777216 | tf_op jit(solution)/shard_map/all_to_all | solution.py:83
  27.2 1.0 copy.14
  28.2 181.0 %all-to-all-done = bf16[64,128,512]{2,1,0:T(8,128)(2,1)} async-done(((bf16[64,128,512]{2,1,0:T(8,128)(2,1)}), bf16[64,128,512]{2,1,0:T(8,128)(2,1)}, u32[]{:S(2)}, u32[]{:S(2)}) %all-to-all-start) | async-done | bytes 8388640 | tf_op jit(solution)/shard_map/all_to_all | solution.py:83
  209.2 5.4 broadcast_in_dim.46
  214.6 10.4 %all-to-all-start.1 = ((bf16[64,128,512]{1,2,0:T(8,128)(2,1)}), bf16[64,128,512]{1,2,0:T(8,128)(2,1)}, u32[]{:S(2)}, u32[]{:S(2)}) async-start(bf16[64,128,512]{1,2,0:T(8,128)(2,1)} %bitcast.46), calls=%async_computation.1 | async-start | bytes 16777216 | tf_op jit(solution)/shard_map/all_to_all | solution.py:84
  228.9 3.6 fusion.16
  232.5 174.8 %all-to-all-done.1 = bf16[64,128,512]{1,2,0:T(8,128)(2,1)} async-done(((bf16[64,128,512]{1,2,0:T(8,128)(2,1)}), bf16[64,128,512]{1,2,0:T(8,128)(2,1)}, u32[]{:S(2)}, u32[]{:S(2)}) %all-to-all-start.1) | async-done | bytes 8388640 | tf_op jit(solution)/shard_map/all_to_all | solution.py:84
  407.4 11.9 %copy.15 = bf16[64,128,512]{2,1,0:T(8,128)(2,1)} copy(bf16[64,128,512]{1,2,0:T(8,128)(2,1)} %all-to-all-done.1) | data formatting | bytes 16777216 | tf_op jit(solution)/shard_map/all_to_all | solution.py:84
  419.3 5.1 fusion.17
  424.4 6.5 %fusion.24 = f32[]{:T(128)} fusion(bf16[8192,512]{1,0:T(8,128)(2,1)S(1)} %bitcast.49, s32[]{:T(128)S(6)} %select_n.32, bf16[8192,512]{1,0:T(8,128)(2,1)} %bitcast.5), kind=kOutput, calls=%fused_computation.22 | convolution fusion | flops 3221749760 | bytes 12583940 | tf_op jit(solution)/shard_map/dot_general | solution.py:45
  431.0 16.6 %while.10 = (s32[]{:T(128)}, f32[3]{0:T(128)S(1)}, s32[3]{0:T(128)S(1)}, s32[2048]{0:T(1024)S(1)}, bf16[2048,512]{1,0:T(8,128)(2,1)}, /*index=5*/bf16[2048,512]{1,0:T(8,128)(2,1)S(1)}, s32[]{:T(128)}) while((s32[]{:T(128)}, f32[3]{0:T(128)S(1)}, s32[3]{0:T(128)S(1)}, s32[2048]{0:T(1024)S(1)}, bf16[2048,512]{1,0:T(8,128)(2,1)}, ...), condition=%wide.region_6.7_spmd, body=%wide.region_4.6_spmd.sunk | while | flops 1075316736 | bytes 4206709 | solution.py:35
  432.1 3.7 fusion.47
  435.9 0.7 dynamic_update_slice.5
  437.7 3.7 fusion.47
  441.4 0.7 dynamic_update_slice.5
  443.2 3.7 fusion.47
  447.0 0.7 dynamic_update_slice.5
  448.3 127.6 %psum.14 = f32[3]{0:T(128)S(1)} all-reduce(f32[3]{0:T(128)S(1)} %compare_select_fusion), channel_id=1, replica_groups=mesh['dp'=4,'seq'=64] {'seq'}, use_global_device_ids=true, to_apply=%region_7.8 | all-reduce | flops 3 | bytes 24 | tf_op jit(solution)/shard_map/psum | solution.py:19
  577.5 9.2 %fusion.23 = f32[512,512]{0,1:T(8,128)} fusion(bf16[64,128,512]{2,1,0:T(8,128)(2,1)} %all-to-all-done, bf16[64,128,512]{1,2,0:T(8,128)(2,1)} %all-to-all-done.1, f32[64,128]{1,0:T(8,128)S(1)} %bitcast.55), kind=kOutput, calls=%fused_computation.21 | convolution fusion | flops 4307550208 | bytes 17858560 | tf_op jit(solution)/shard_map/dot_general | solution.py:98
  587.2 45.8 %all-reduce.2.cloned.1.call-done = f32[512,512]{0,1:T(8,128)} async-done(((f32[512,512]{0,1:T(8,128)}), f32[512,512]{0,1:T(8,128)}) %all-reduce.2.cloned.1.call-update) | async-done | bytes 1048592 | tf_op jit(solution)/shard_map/psum | solution.py:97
  633.0 1.0 multiply_bitcast_fusion
  633.9 0.8 copy.16
  (27 shorter events, 7.5 us)
Async XLA Ops:
  13.3 13.5 %copy-start.1 = (bf16[128,4096]{1,0:T(8,128)(2,1)S(1)}, bf16[128,4096]{1,0:T(8,128)(2,1)}, u32[]{:S(2)}) copy-start(bf16[128,4096]{1,0:T(8,128)(2,1)} %param.6) | copy-start | bytes 3145732
  13.3 195.9 %all-to-all-start = ((bf16[64,128,512]{2,1,0:T(8,128)(2,1)}), bf16[64,128,512]{2,1,0:T(8,128)(2,1)}, u32[]{:S(2)}, u32[]{:S(2)}) async-start(bf16[64,128,512]{2,1,0:T(8,128)(2,1)} %bitcast.47), calls=%async_computation | async-start | bytes 16777216 | tf_op jit(solution)/shard_map/all_to_all | solution.py:83
  214.6 10.6 %copy-start.2 = (s32[1,3]{1,0:T(1,128)S(1)}, s32[1,3]{1,0:T(1,128)}, u32[]{:S(2)}) copy-start(s32[1,3]{1,0:T(1,128)} %param.7) | copy-start | bytes 40
  214.6 192.8 %all-to-all-start.1 = ((bf16[64,128,512]{1,2,0:T(8,128)(2,1)}), bf16[64,128,512]{1,2,0:T(8,128)(2,1)}, u32[]{:S(2)}, u32[]{:S(2)}) async-start(bf16[64,128,512]{1,2,0:T(8,128)(2,1)} %bitcast.46), calls=%async_computation.1 | async-start | bytes 16777216 | tf_op jit(solution)/shard_map/all_to_all | solution.py:84
  225.0 408.0 %all-reduce.2.cloned.1.call-start = ((), (), s32[]{:S(2)}) async-start(), calls=%async_computation.2 | async-start | bytes 2097152 | tf_op jit(solution)/shard_map/psum | solution.py:97
  419.3 5.1 copy-start
Sparse Core Ops, SparseCore 0:
  586.8 46.1 all-reduce.1
where the time goes:
time: 643 us; the launch traced here: 642 us
  waiting for transfers between devices  402 us (63%)
  blocking collectives  128 us (20%)
  local copies, waits for them, and re-layouts  29.5 us (5%)
  matrix products  27.2 us (4%)
  starting transfers between devices  24.1 us (4%)
  between operations  17.4 us (3%)
  other arithmetic  14.2 us (2%)
    all_to_all x1, waiting for transfers between devices, body(): lax.all_to_all(act_pieces, 'seq', split_axis=0, concat_axis=0, tiled=True)  181 us
    all_to_all x1, waiting for transfers between devices, body(): lax.all_to_all(grad_pieces, 'seq', split_axis=0, concat_axis=0, tiled=True)  175 us
    psum x1, blocking collectives, clip_factors(): totals = lax.psum(partial_value, 'seq')  128 us
    psum x1, waiting for transfers between devices, body(): lax.psum(lax.dot_general(flat_acts, scaled_grads, (((0,), (0,)), ((), ())...  45.8 us
    all_to_all x1, starting transfers between devices, body(): lax.all_to_all(act_pieces, 'seq', split_axis=0, concat_axis=0, tiled=True)  13.5 us
  transfers between devices with their start and end apart: 3, of which 3 were waited for; matrix products, arithmetic and copies ran while one was open for 1% of the time, Pallas kernels for 0%

commit v1 on v0

v1 whole, which is shorter than its diff:
```python
import functools

import jax
import jax.numpy as jnp
from jax import lax
from jax.experimental import pallas as pl
from jax.experimental.pallas import tpu as pltpu
from jax.sharding import Mesh, PartitionSpec as P

DOCS = 3
NZ, NY, NC = 8, 4, 2
TOK = 128
BLOCKS = NY * NC
CHUNK = TOK * BLOCKS
TILE = 512
WIDE = TILE // 2
LANES = 128
MEMBERS = NZ * BLOCKS
SEQ = ("z", "y", "core")
F32, BF16 = jnp.float32, jnp.bfloat16
MIB = 1 << 20
STEPS = (0, -1, 1, -2, 2, -3, 3, 4)
VMEM = pl.BlockSpec(memory_space=pltpu.VMEM)
SMEM = pl.BlockSpec(memory_space=pltpu.SMEM)
ANY = pl.BlockSpec(memory_space=pl.ANY)


def in_hbm(x):
    return pltpu.with_memory_space_constraint(x, pltpu.HBM)


def ring(n, k):
    return [(i, (i + k) % n) for i in range(n)]


def split_mesh(mesh):
    dp = mesh.devices.shape[0]
    return Mesh(mesh.devices.reshape(dp, NZ, NY, NC), ("dp",) + SEQ)


def params(mib):
    return pltpu.CompilerParams(vmem_limit_bytes=mib * MIB)


def cost(flops, moved):
    return pl.CostEstimate(flops=flops, bytes_accessed=moved, transcendentals=0)


def open_acts_kernel(acts_ref, units_in, out_ref, z_ref, doc_ref, buf, units_ref, sem, units_sem):
    fetch = pltpu.make_async_copy(units_in, units_ref, units_sem)
    fetch.start()
    copies = [
        pltpu.make_async_copy(acts_ref.at[:, pl.ds(i * TILE, TILE)], buf.at[i], sem.at[i])
        for i in range(NZ)
    ]
    for copy in copies:
        copy.start()
    fetch.wait()
    z, y, core = (lax.axis_index(a) for a in SEQ)
    first_end = units_ref[0, 0]
    second_end = first_end + units_ref[0, 1]
    for s, step in enumerate(STEPS):
        there = lax.rem(z + (step + NZ), NZ)
        z_ref[s] = there
        for b in range(BLOCKS):
            unit = there * BLOCKS + lax.rem(y + (NY - b // NC), NY) * NC + (core if b % NC == 0 else 1 - core)
            doc_ref[s * BLOCKS + b] = (unit >= first_end).astype(jnp.int32) + (
                unit >= second_end
            ).astype(jnp.int32)
    for i in range(NZ):
        copies[i].wait()
        out_ref[i] = buf[i].T


def open_acts(acts, units):
    return pl.pallas_call(
        open_acts_kernel,
        in_specs=[ANY, ANY],
        out_specs=[VMEM, SMEM, SMEM],
        out_shape=[
            jax.ShapeDtypeStruct((NZ, TILE, TOK), BF16),
            jax.ShapeDtypeStruct((NZ,), jnp.int32),
            jax.ShapeDtypeStruct((MEMBERS,), jnp.int32),
        ],
        scratch_shapes=[
            pltpu.VMEM((NZ, TOK, TILE), BF16),
            pltpu.SMEM((1, DOCS), jnp.int32),
            pltpu.SemaphoreType.DMA((NZ,)),
            pltpu.SemaphoreType.DMA,
        ],
        compiler_params=params(8),
        cost_estimate=cost(0, 2 * MIB),
        name="open_acts",
    )(in_hbm(acts), in_hbm(units))


def open_grads_kernel(grads_ref, kept_ref, given_ref, sem):
    y, core = lax.axis_index("y"), lax.axis_index("core")
    copies = []
    for j, (out, c) in enumerate(((given_ref, 1 - core), (kept_ref, core))):
        for k in range(NY):
            tile = lax.rem(y + k, NY) * NC + c
            for h in range(2):
                cols = pl.ds(pl.multiple_of(tile * TILE + h * WIDE, WIDE), WIDE)
                copies.append(
                    pltpu.make_async_copy(grads_ref.at[:, cols], out.at[k, h], sem.at[j, k, h])
                )
    for copy in copies:
        copy.start()
    for copy in copies:
        copy.wait()


def open_grads(grads):
    shape = jax.ShapeDtypeStruct((NY, 2, TOK, WIDE), BF16)
    return pl.pallas_call(
        open_grads_kernel,
        in_specs=[ANY],
        out_specs=[VMEM] * 2,
        out_shape=[shape] * 2,
        scratch_shapes=[pltpu.SemaphoreType.DMA((NC, NY, 2))],
        compiler_params=params(4),
        cost_estimate=cost(0, 2 * MIB),
        name="open_grads",
    )(in_hbm(grads))


def pair_kernel(kept_ref, got_ref, *outs):
    for k in range(NY):
        for h in range(2):
            outs[k][h, 0] = kept_ref[k, h]
            outs[k][h, 1] = got_ref[k, h]


def pair_up(kept, got):
    return pl.pallas_call(
        pair_kernel,
        in_specs=[VMEM] * 2,
        out_specs=[VMEM] * NY,
        out_shape=[jax.ShapeDtypeStruct((2, NC, TOK, WIDE), BF16)] * NY,
        compiler_params=params(8),
        cost_estimate=cost(0, 2 * MIB),
        name="pair_up",
    )(kept, got)


def join_kernel(*refs):
    for h in range(2):
        for k in range(NY):
            refs[NY][h, k * NC : (k + 1) * NC] = refs[k][h]


def join(pairs):
    return pl.pallas_call(
        join_kernel,
        in_specs=[VMEM] * NY,
        out_specs=VMEM,
        out_shape=jax.ShapeDtypeStruct((2, BLOCKS, TOK, WIDE), BF16),
        compiler_params=params(8),
        cost_estimate=cost(0, 2 * MIB),
        name="join",
    )(*pairs)


PIECES = (
    (0, 0, TILE),
    (1, 0, TILE),
    (2, 0, TILE),
    (3, 0, TILE),
    (4, 0, WIDE),
    (4, WIDE, WIDE),
    (5, 0, WIDE),
    (5, WIDE, WIDE),
    (6, 0, TILE),
    (7, 0, TILE),
)
ACTS = len(PIECES)


def acts_copies(acts, z, buf, sem):
    return [
        pltpu.make_async_copy(ref.at[z], buf.at[b, pl.ds(row, rows)], sem.at[i])
        for i, (ref, (b, row, rows)) in enumerate(zip(acts, PIECES))
    ]


def side_by_side(buf):
    return jnp.concatenate([buf[b] for b in range(BLOCKS)], axis=1)


def norm_kernel(chunks, has_acc, is_last, z_ref, doc_ref, *refs):
    n = len(chunks)
    acts, refs = refs[:ACTS], refs[ACTS:]
    many = 2 if is_last else n
    grads, refs = refs[:many], refs[many:]
    if has_acc and not is_last:
        refs = refs[1:]
    acc_ref, refs = refs[0], refs[1:]
    if is_last:
        out_ref, refs = refs[0], refs[1:]
        acts_buf, sem = refs
    else:
        acts_buf, grads_buf, sem = refs
    copies = []
    for i, s in enumerate(chunks):
        copies.append(acts_copies(acts, z_ref[s], acts_buf.at[i], sem.at[i]))
        if not is_last:
            copies[-1].append(
                pltpu.make_async_copy(grads[i], grads_buf.at[i], sem.at[i, ACTS])
            )
    for several in copies:
        for copy in several:
            copy.start()
    if not has_acc:
        acc_ref[...] = jnp.zeros_like(acc_ref)
    for i, s in enumerate(chunks):
        for copy in copies[i]:
            copy.wait()
        for d in range(DOCS):
            held = [doc_ref[s * BLOCKS + b] == d for b in range(BLOCKS)]

            @pl.when(functools.reduce(jnp.logical_or, held))
            def _():
                x = side_by_side(acts_buf.at[i])
                for h in range(2):
                    g = grads[h] if is_last else grads_buf.at[i, h]
                    kept = [
                        jnp.where(held[b], g[b], jnp.zeros((TOK, WIDE), BF16))
                        for b in range(BLOCKS)
                    ]
                    acc_ref[d, :, h * WIDE : (h + 1) * WIDE] += jnp.dot(
                        x, jnp.concatenate(kept, axis=0), preferred_element_type=F32
                    )

    if is_last:
        lane = lax.broadcasted_iota(jnp.int32, (1, LANES), 1)
        row = jnp.zeros((1, LANES), F32)
        for d in range(DOCS):
            total = acc_ref[d]
            row = jnp.where(lane == d, jnp.sum(total * total), row)
        out_ref[...] = jnp.broadcast_to(row[None], out_ref.shape)


def norm_call(chunks, z_list, docs, acts, grads, acc=None, is_last=False):
    n = len(chunks)
    operands = [z_list, docs, *map(in_hbm, acts)]
    for s in chunks:
        operands += grads[s] if is_last else [in_hbm(grads[s])]
    in_specs = [SMEM] * 2 + [ANY] * ACTS + ([VMEM] * 2 if is_last else [ANY] * n)
    aliases = {}
    if acc is not None:
        operands.append(acc)
        in_specs.append(VMEM)
        if not is_last:
            aliases = {len(operands) - 1: 0}
    scratch = [pltpu.VMEM((n, BLOCKS, TILE, TOK), BF16)]
    if is_last:
        out_shape = jax.ShapeDtypeStruct((MEMBERS, 1, LANES), F32)
    else:
        out_shape = jax.ShapeDtypeStruct((DOCS, TILE, TILE), F32)
        scratch.append(pltpu.VMEM((n, 2, BLOCKS, TOK, WIDE), BF16))
    return pl.pallas_call(
        functools.partial(norm_kernel, chunks, acc is not None, is_last),
        in_specs=in_specs,
        out_specs=VMEM,
        out_shape=out_shape,
        input_output_aliases=aliases,
        scratch_shapes=scratch + [pltpu.SemaphoreType.DMA((n, ACTS + 2))],
        compiler_params=params(12 + 2 * n),
        cost_estimate=cost(2 * n * CHUNK * TILE * TILE, 3 * n * MIB),
        name="norm_" + "_".join(str(s) for s in chunks),
    )(*operands)


def grad_kernel(z_ref, doc_ref, norm_ref, *refs):
    acts, refs = refs[:ACTS], refs[ACTS:]
    grads, refs = refs[: NZ + 1], refs[NZ + 1 :]
    outs, ratio_ref, acc_ref, acts_buf, grads_buf, sem = refs[:4], *refs[4:]
    copies = []
    for s in range(NZ):
        if s < NZ - 1:
            pieces = [(grads[s], grads_buf.at[s])]
        else:
            pieces = [(grads[s + h], grads_buf.at[s, h]) for h in range(2)]
        copies.append(
            [
                pltpu.make_async_copy(src, dst, sem.at[s, ACTS + i])
                for i, (src, dst) in enumerate(pieces)
            ]
            + acts_copies(acts, z_ref[s], acts_buf.at[s], sem.at[s])
        )
        for copy in copies[s]:
            copy.start()
    squares = jnp.sum(norm_ref[...], axis=0)
    doc_norm = jnp.where(squares > 0, jnp.sqrt(squares), 0)
    lane = lax.broadcasted_iota(jnp.int32, (1, LANES), 1)
    threshold = jnp.sum(doc_norm, axis=1, keepdims=True) / DOCS
    ratio_ref[...] = doc_norm / threshold
    factor = 1.0 / jnp.maximum(doc_norm, threshold)
    clip = [jnp.sum(jnp.where(lane == d, factor, 0)) for d in range(DOCS)]
    for s in range(NZ):
        for copy in copies[s]:
            copy.wait()
        for h in range(2):
            scaled = []
            for b in range(BLOCKS):
                doc = doc_ref[s * BLOCKS + b]
                mine = jnp.where(doc == 0, clip[0], jnp.where(doc == 1, clip[1], clip[2]))
                scaled.append((mine * grads_buf[s, h, b].astype(F32)).astype(BF16))
            product = jnp.dot(
                side_by_side(acts_buf.at[s]),
                jnp.concatenate(scaled, axis=0),
                preferred_element_type=F32,
            )
            cols = slice(h * WIDE, (h + 1) * WIDE)
            if s == 0:
                acc_ref[:, cols] = product
            else:
                acc_ref[:, cols] += product
    me = lax.axis_index("dp")
    for k in range(4):
        first = pl.multiple_of(lax.rem(me + k, 4) * TOK, TOK)
        outs[k][...] = acc_ref[pl.ds(first, TOK), :]


def grad_call(z_list, docs, norms, acts, grads):
    operands = [z_list, docs, norms, *map(in_hbm, acts)]
    operands += map(in_hbm, [*grads[:-1], *grads[-1]])
    return pl.pallas_call(
        grad_kernel,
        in_specs=[SMEM] * 2 + [VMEM] + [ANY] * (ACTS + NZ + 1),
        out_specs=[VMEM] * 5,
        out_shape=[jax.ShapeDtypeStruct((TOK, TILE), F32)] * 4
        + [jax.ShapeDtypeStruct((1, LANES), F32)],
        scratch_shapes=[
            pltpu.VMEM((TILE, TILE), F32),
            pltpu.VMEM((NZ, BLOCKS, TILE, TOK), BF16),
            pltpu.VMEM((NZ, 2, BLOCKS, TOK, WIDE), BF16),
            pltpu.SemaphoreType.DMA((NZ, ACTS + 2)),
        ],
        compiler_params=params(32),
        cost_estimate=cost(2 * NZ * CHUNK * TILE * TILE, 18 * MIB),
        name="grad",
    )(*operands)


def body(hidden_states, q_grads, doc_units):
    def after(x, *done):
        return lax.optimization_barrier((x, *done))[0]

    def move(x, axis, k):
        return lax.ppermute(x, axis, ring(lax.axis_size(axis), k))


    kept, given = open_grads(q_grads)
    got = move(given, "core", 1)
    pair = pair_up(kept, got)
    near = {k: move(pair[k], "y", k) for k in (2, 1, 3)}
    here = join([pair[0], near[1], near[2], near[3]])

    acts_t, z_list, docs = open_acts(hidden_states, doc_units)
    own = lax.all_to_all(acts_t, "z", split_axis=0, concat_axis=0, tiled=True)

    g = {0: here}
    right, left = move(own, "y", 1), move(own, "y", -1)
    own_c = move(own, "core", 1)
    for s in (1, 2):
        g[-s], g[s] = move(g[1 - s], "z", 1), move(g[s - 1], "z", -1)
    g[-3] = move(after(g[-2], right, left), "z", 1)
    g[3] = move(after(g[2], right, left), "z", -1)
    far = [move(right[:, :WIDE], "y", 1), move(left[:, WIDE:], "y", -1)]
    right_c, left_c = move(right, "core", 1), move(left, "core", 1)
    last = [
        move(after(g[-3][0], *far, right_c, left_c), "z", 1),
        move(after(g[3][1], *far, right_c, left_c), "z", -1),
    ]
    acts = [own, own_c, right, right_c, *far, *(move(x, "core", 1) for x in far), left, left_c]
    chunks = [g[s] for s in STEPS[:-1]] + [last]
    acc = norm_call((0, 1, 2, 3, 4, 5, 6), z_list, docs, acts, chunks)
    partial = norm_call((7,), z_list, docs, acts, chunks, acc, is_last=True)
    norms = lax.all_to_all(partial, SEQ, split_axis=0, concat_axis=0, tiled=True)

    *parts, ratio = grad_call(z_list, docs, norms, acts, chunks)
    total = parts[0]
    for k in (2, 1, 3):
        total = total + move(parts[k], "dp", k)
    return (ratio[:, :DOCS], (total * (4096 / 12))[None])


def solution(mesh):
    in_specs = (P(("dp",) + SEQ, None), P(("dp",) + SEQ, None), P("dp", None))
    out_specs = (P("dp", None), P(SEQ, "dp", None))
    return jax.shard_map(
        body, mesh=split_mesh(mesh), in_specs=in_specs, out_specs=out_specs, check_vma=False
    )
```

time: 643 us -> 179 us (0.28)
  waiting for transfers between devices: 402 us -> 84.2 us
  blocking collectives: 128 us -> 20.1 us
  local copies, waits for them, and re-layouts: 29.5 us -> 1.54 us
  matrix products: 27.2 us -> 0 us
  Pallas kernels: 0 us -> 24.7 us
  starting transfers between devices: 24.1 us -> 46.4 us
  between operations: 17.4 us -> 0.93 us
  other arithmetic: 14.2 us -> 0.8 us
    all_to_all x2 -> x1, waiting for transfers between devices: 356 us -> 6.24 us  [body(): own = lax.all_to_all(acts_t, 'z', split_axis=0, concat_axis=0, tiled=True)]
    psum x1 -> x0, blocking collectives: 128 us -> none  [clip_factors(): totals = lax.psum(partial_value, 'seq')]
    ppermute x0 -> x24, waiting for transfers between devices: none -> 77.9 us  [move(): return lax.ppermute(x, axis, ring(lax.axis_size(axis), k))]
    psum x1 -> x0, waiting for transfers between devices: 45.8 us -> none  [body(): lax.psum(lax.dot_general(flat_acts, scaled_grads, (((0,), (0,)), ((), ())...]
    ppermute x0 -> x24, starting transfers between devices: none -> 37.4 us  [move(): return lax.ppermute(x, axis, ring(lax.axis_size(axis), k))]
    dot_general x6 -> x0, matrix products: 27.2 us -> none  [the longest x3 11.2 us: doc_square(): lax.dot_general(flat_acts, doc_grads, (((0,), (0,)), ((), ())), preferred...]
    pallas_call x0 -> x7, Pallas kernels: none -> 24.7 us  [the longest x2 12.3 us: norm_call(): pl.pallas_call(functools.partial(norm_kernel, chunks, acc is not None, is...]
    all_to_all x0 -> x1, blocking collectives: none -> 20.1 us  [body(): lax.all_to_all(partial, SEQ, split_axis=0, concat_axis=0, tiled=True)]
  transfers between devices with their start and end apart: 3 -> 25, of which waited for: 3 -> 13; matrix products, arithmetic and copies ran while one was open for 1% -> 0% of each run, Pallas kernels for 0% -> 6%
where the time goes in v1:
time: 179 us
  waiting for transfers between devices  84.2 us (47%)
  starting transfers between devices  46.4 us (26%)
  Pallas kernels  24.7 us (14%)
  blocking collectives  20.1 us (11%)
    ppermute x24, waiting for transfers between devices, move(): return lax.ppermute(x, axis, ring(lax.axis_size(axis), k))  77.9 us
    ppermute x24, starting transfers between devices, move(): return lax.ppermute(x, axis, ring(lax.axis_size(axis), k))  37.4 us
    all_to_all x1, blocking collectives, body(): lax.all_to_all(partial, SEQ, split_axis=0, concat_axis=0, tiled=True)  20.1 us
    pallas_call x2, Pallas kernels, norm_call(): pl.pallas_call(functools.partial(norm_kernel, chunks, acc is not None, is...  12.3 us
    all_to_all x1, starting transfers between devices, body(): own = lax.all_to_all(acts_t, 'z', split_axis=0, concat_axis=0, tiled=True)  9.03 us
    pallas_call x1, Pallas kernels, grad_call(): pl.pallas_call(grad_kernel, in_specs=[SMEM] * 2 + [VMEM] + [ANY] * (ACTS...  8.07 us
    all_to_all x1, waiting for transfers between devices, body(): own = lax.all_to_all(acts_t, 'z', split_axis=0, concat_axis=0, tiled=True)  6.24 us
  transfers between devices with their start and end apart: 25, of which 13 were waited for; matrix products, arithmetic and copies ran while one was open for 0% of the time, Pallas kernels for 6%

profile of v1, /device:TPU:1, one launch (start us, length us, event | category | flops | bytes accessed | tf_op | source)
XLA Modules:
  0.0 178.6 jit_solution(7022214689705403906)
XLA Ops:
  0.6 2.8 %open_acts.1 = (bf16[8,512,128]{2,1,0:T(8,128)(2,1)}, s32[8]{0:T(128)S(1)}, s32[64]{0:T(128)S(1)}) custom-call(bf16[128,4096]{1,0:T(8,128)(2,1)} %acts_ref.1, s32[1,3]{1,0:T(1,128)} %units_in.1), custom_call_target="tpu_custom_call" | custom-call | bytes 2097152 | tf_op jit(solution)/shard_map/open_acts/pallas_call | solution.py:76
  3.4 9.0 %all-to-all-start = ((bf16[8,512,128]{2,1,0:T(8,128)(2,1)}), bf16[8,512,128]{2,1,0:T(8,128)(2,1)S(1)}, u32[]{:S(2)}, u32[]{:S(2)}) async-start(bf16[8,512,128]{2,1,0:T(8,128)(2,1)} %get-tuple-element.22), calls=%async_computation | async-start | bytes 2097152 | tf_op jit(solution)/shard_map/all_to_all | solution.py:362
  21.5 3.9 %collective-permute-done.10.refs_1_ = bf16[2,2,128,256]{3,2,1,0:T(8,128)(2,1)S(1)} collective-permute-done((bf16[2,2,128,256]{3,2,1,0:T(8,128)(2,1)S(1)}, bf16[2,2,128,256]{3,2,1,0:T(8,128)(2,1)S(1)}, u32[]{:S(2)}, u32[]{:S(2)}) %collective-permute-start.10) | collective-permute-done | bytes 262176 | tf_op jit(solution)/shard_map/ppermute | solution.py:352
  25.4 6.7 %collective-permute-done.11.refs_2_ = bf16[2,2,128,256]{3,2,1,0:T(8,128)(2,1)S(1)} collective-permute-done((bf16[2,2,128,256]{3,2,1,0:T(8,128)(2,1)S(1)}, bf16[2,2,128,256]{3,2,1,0:T(8,128)(2,1)S(1)}, u32[]{:S(2)}, u32[]{:S(2)}) %collective-permute-start.11) | collective-permute-done | bytes 262176 | tf_op jit(solution)/shard_map/ppermute | solution.py:352
  32.2 3.0 %collective-permute-start.17 = (bf16[2,8,128,256]{3,2,1,0:T(8,128)(2,1)S(1)}, bf16[2,8,128,256]{3,2,1,0:T(8,128)(2,1)S(1)}, u32[]{:S(2)}, u32[]{:S(2)}) collective-permute-start(bf16[2,8,128,256]{3,2,1,0:T(8,128)(2,1)S(1)} %join.1.refs_10_), channel_id=1, source_target_pairs={{0,56},{8,0},{16,8},{24,16},{32,24},{40,32},{48,40},{56,48},{1,57}... | collective-permute-start | bytes 3145736 | tf_op jit(solution)/shard_map/ppermute | solution.py:352
  35.3 6.2 %all-to-all-done.refs_0_ = bf16[8,512,128]{2,1,0:T(8,128)(2,1)S(1)} async-done(((bf16[8,512,128]{2,1,0:T(8,128)(2,1)}), bf16[8,512,128]{2,1,0:T(8,128)(2,1)S(1)}, u32[]{:S(2)}, u32[]{:S(2)}) %all-to-all-start) | async-done | bytes 1048608 | tf_op jit(solution)/shard_map/all_to_all | solution.py:362
  44.1 14.9 %collective-permute-done.17.refs_12_ = bf16[2,8,128,256]{3,2,1,0:T(8,128)(2,1)S(1)} collective-permute-done((bf16[2,8,128,256]{3,2,1,0:T(8,128)(2,1)S(1)}, bf16[2,8,128,256]{3,2,1,0:T(8,128)(2,1)S(1)}, u32[]{:S(2)}, u32[]{:S(2)}) %collective-permute-start.17) | collective-permute-done | bytes 1048608 | tf_op jit(solution)/shard_map/ppermute | solution.py:352
  59.0 3.3 %collective-permute-start.18 = (bf16[2,8,128,256]{3,2,1,0:T(8,128)(2,1)S(1)}, bf16[2,8,128,256]{3,2,1,0:T(8,128)(2,1)S(1)}, u32[]{:S(2)}, u32[]{:S(2)}) collective-permute-start(bf16[2,8,128,256]{3,2,1,0:T(8,128)(2,1)S(1)} %collective-permute-done.17.refs_12_), channel_id=1, source_target_pairs={{0,56},{8,0},{16,8},{24,16},{32,24},{40,32},{48,40},{56,48},{1,57}... | collective-permute-start | bytes 3145736 | tf_op jit(solution)/shard_map/ppermute | solution.py:352
  62.3 3.3 %collective-permute-done.4.refs_8_ = bf16[8,512,128]{2,1,0:T(8,128)(2,1)S(1)} collective-permute-done((bf16[8,512,128]{2,1,0:T(8,128)(2,1)S(1)}, bf16[8,512,128]{2,1,0:T(8,128)(2,1)S(1)}, u32[]{:S(2)}, u32[]{:S(2)}) %collective-permute-start.4) | collective-permute-done | bytes 1048608 | tf_op jit(solution)/shard_map/ppermute | solution.py:352
  65.6 3.5 %collective-permute-start.5 = (bf16[8,256,128]{2,1,0:T(8,128)(2,1)S(1)}, bf16[8,256,128]{2,1,0:T(8,128)(2,1)S(1)}, u32[]{:S(2)}, u32[]{:S(2)}) collective-permute-start(bf16[8,256,128]{2,1,0:T(8,128)(2,1)S(1)} %slice.21), channel_id=1, source_target_pairs={{0,6},{2,0},{4,2},{6,4},{1,7},{3,1},{5,3},{7,5},{8,14},{10,8},{12,... | collective-permute-start | bytes 1572872 | tf_op jit(solution)/shard_map/ppermute | solution.py:352
  69.1 14.5 %collective-permute-done.18.refs_14_ = bf16[2,8,128,256]{3,2,1,0:T(8,128)(2,1)S(1)} collective-permute-done((bf16[2,8,128,256]{3,2,1,0:T(8,128)(2,1)S(1)}, bf16[2,8,128,256]{3,2,1,0:T(8,128)(2,1)S(1)}, u32[]{:S(2)}, u32[]{:S(2)}) %collective-permute-start.18) | collective-permute-done | bytes 1048608 | tf_op jit(solution)/shard_map/ppermute | solution.py:352
  85.7 3.4 %collective-permute-start.19 = (bf16[2,8,128,256]{3,2,1,0:T(8,128)(2,1)S(1)}, bf16[2,8,128,256]{3,2,1,0:T(8,128)(2,1)S(1)}, u32[]{:S(2)}, u32[]{:S(2)}) collective-permute-start(bf16[2,8,128,256]{3,2,1,0:T(8,128)(2,1)S(1)} %collective-permute-done.18.refs_14_), channel_id=1, source_target_pairs={{0,56},{8,0},{16,8},{24,16},{32,24},{40,32},{48,40},{56,48},{1,57}... | collective-permute-start | bytes 3145736 | tf_op jit(solution)/shard_map/ppermute | solution.py:352
  91.1 13.4 %collective-permute-done.3.refs_4_ = bf16[8,256,128]{2,1,0:T(8,128)(2,1)S(1)} collective-permute-done((bf16[8,256,128]{2,1,0:T(8,128)(2,1)S(1)}, bf16[8,256,128]{2,1,0:T(8,128)(2,1)S(1)}, u32[]{:S(2)}, u32[]{:S(2)}) %collective-permute-start.3) | collective-permute-done | bytes 524320 | tf_op jit(solution)/shard_map/ppermute | solution.py:352
  105.4 6.3 %collective-permute-done.19.refs_16_ = bf16[2,8,128,256]{3,2,1,0:T(8,128)(2,1)S(1)} collective-permute-done((bf16[2,8,128,256]{3,2,1,0:T(8,128)(2,1)S(1)}, bf16[2,8,128,256]{3,2,1,0:T(8,128)(2,1)S(1)}, u32[]{:S(2)}, u32[]{:S(2)}) %collective-permute-start.19) | collective-permute-done | bytes 1048608 | tf_op jit(solution)/shard_map/ppermute | solution.py:352
  112.5 3.5 %collective-permute-start.20 = (bf16[8,128,256]{2,1,0:T(8,128)(2,1)S(1)}, bf16[8,128,256]{2,1,0:T(8,128)(2,1)S(1)}, u32[]{:S(2)}, u32[]{:S(2)}) collective-permute-start(bf16[8,128,256]{2,1,0:T(8,128)(2,1)S(1)} %slice_bitcast_fusion), channel_id=1, source_target_pairs={{0,56},{8,0},{16,8},{24,16},{32,24},{40,32},{48,40},{56,48},{1,57}... | collective-permute-start | bytes 1572872 | tf_op jit(solution)/shard_map/ppermute | solution.py:352
  118.5 9.1 %norm_0_1_2_3_4_5_6.1.refs_12_ = f32[3,512,512]{2,1,0:T(8,128)S(1)} custom-call(s32[8]{0:T(128)S(1)} %get-tuple-element.20.z_ref, s32[64]{0:T(128)S(1)} %get-tuple-element.21.doc_ref, bf16[8,512,128]{2,1,0:T(8,128)(2,1)} %copy-done.3, bf16[8,512,128]{2,1,0:T(8,128)(2,1)} %copy-done.8, bf16[8,512,128]{2,1,0:T(8,128)(2,1)} %copy-done.5, ...), custom_call_target="tpu_custom_call" | custom-call | flops 3758096384 | bytes 22020096 | tf_op jit(solution)/shard_map/norm_0_1_2_3_4_5_6/pallas_call | solution.py:262
  127.6 2.8 %collective-permute-done.16.refs_10_.refs_17_ = bf16[8,128,256]{2,1,0:T(8,128)(2,1)S(1)} collective-permute-done((bf16[8,128,256]{2,1,0:T(8,128)(2,1)S(1)}, bf16[8,128,256]{2,1,0:T(8,128)(2,1)S(1)}, u32[]{:S(2)}, u32[]{:S(2)}) %collective-permute-start.16) | collective-permute-done | bytes 524320 | tf_op jit(solution)/shard_map/ppermute | solution.py:352
  130.5 3.2 %norm_7.1 = f32[64,1,128]{2,1,0:T(1,128)S(1)} custom-call(s32[8]{0:T(128)S(1)} %get-tuple-element.20.z_ref, s32[64]{0:T(128)S(1)} %get-tuple-element.21.doc_ref, bf16[8,512,128]{2,1,0:T(8,128)(2,1)} %copy-done.3, bf16[8,512,128]{2,1,0:T(8,128)(2,1)} %copy-done.8, bf16[8,512,128]{2,1,0:T(8,128)(2,1)} %copy-done.5, bf16[8,512,128]{2,1,0:T(8,128)(2,1)} %copy-done.7, ...), custom_call_target="tpu_custom_call" | custom-call | flops 536870912 | bytes 3145728 | tf_op jit(solution)/shard_map/norm_7/pallas_call | solution.py:262
  133.7 20.1 %all_to_all.10.norm_ref = f32[64,1,128]{2,1,0:T(1,128)S(1)} all-to-all(f32[64,1,128]{2,1,0:T(1,128)S(1)} %norm_7.1), channel_id=1, replica_groups=mesh['dp'=4,'z'=8,'y'=4,'core'=2] {'z','y','core'}, dimensions={0} | all-to-all | bytes 65536 | tf_op jit(solution)/shard_map/all_to_all | solution.py:381
  153.8 8.1 %grad.1 = (f32[128,512]{1,0:T(8,128)S(1)}, f32[128,512]{1,0:T(8,128)S(1)}, f32[128,512]{1,0:T(8,128)S(1)}, f32[128,512]{1,0:T(8,128)S(1)}, f32[1,128]{1,0:T(1,128)}) custom-call(s32[8]{0:T(128)S(1)} %get-tuple-element.20.z_ref, s32[64]{0:T(128)S(1)} %get-tuple-element.21.doc_ref, f32[64,1,128]{2,1,0:T(1,128)S(1)} %all_to_all.10.norm_ref, ...), custom_call_target="tpu_custom_call" | custom-call | flops 4294967296 | bytes 18874368 | tf_op jit(solution)/shard_map/grad/pallas_call | solution.py:329
  161.8 3.5 %collective-permute-start.21 = (f32[128,512]{1,0:T(8,128)S(1)}, f32[128,512]{1,0:T(8,128)S(1)}, u32[]{:S(2)}, u32[]{:S(2)}) collective-permute-start(f32[128,512]{1,0:T(8,128)S(1)} %get-tuple-element.35), channel_id=1, source_target_pairs={{0,128},{64,192},{128,0},{192,64},{1,129},{65,193},{129,1},{193,65... | collective-permute-start | bytes 786440 | tf_op jit(solution)/shard_map/ppermute | solution.py:352
  165.4 2.7 %collective-permute-start.23 = (f32[128,512]{1,0:T(8,128)S(1)}, f32[128,512]{1,0:T(8,128)S(1)}, u32[]{:S(2)}, u32[]{:S(2)}) collective-permute-start(f32[128,512]{1,0:T(8,128)S(1)} %get-tuple-element.37), channel_id=1, source_target_pairs={{0,192},{64,0},{128,64},{192,128},{1,193},{65,1},{129,65},{193,129... | collective-permute-start | bytes 786440 | tf_op jit(solution)/shard_map/ppermute | solution.py:352
  168.1 3.4 %collective-permute-done.21 = f32[128,512]{1,0:T(8,128)S(1)} collective-permute-done((f32[128,512]{1,0:T(8,128)S(1)}, f32[128,512]{1,0:T(8,128)S(1)}, u32[]{:S(2)}, u32[]{:S(2)}) %collective-permute-start.21) | collective-permute-done | bytes 262176 | tf_op jit(solution)/shard_map/ppermute | solution.py:352
  171.5 6.3 %collective-permute-done.22 = f32[128,512]{1,0:T(8,128)S(1)} collective-permute-done((f32[128,512]{1,0:T(8,128)S(1)}, f32[128,512]{1,0:T(8,128)S(1)}, u32[]{:S(2)}, u32[]{:S(2)}) %collective-permute-start.22) | collective-permute-done | bytes 262176 | tf_op jit(solution)/shard_map/ppermute | solution.py:352
  (75 shorter events, 20.7 us)
Async XLA Ops:
  3.4 38.1 %all-to-all-start = ((bf16[8,512,128]{2,1,0:T(8,128)(2,1)}), bf16[8,512,128]{2,1,0:T(8,128)(2,1)S(1)}, u32[]{:S(2)}, u32[]{:S(2)}) async-start(bf16[8,512,128]{2,1,0:T(8,128)(2,1)} %get-tuple-element.22), calls=%async_computation | async-start | bytes 2097152 | tf_op jit(solution)/shard_map/all_to_all | solution.py:362
  16.5 8.9 %collective-permute-start.10 = (bf16[2,2,128,256]{3,2,1,0:T(8,128)(2,1)S(1)}, bf16[2,2,128,256]{3,2,1,0:T(8,128)(2,1)S(1)}, u32[]{:S(2)}, u32[]{:S(2)}) collective-permute-start(bf16[2,2,128,256]{3,2,1,0:T(8,128)(2,1)S(1)} %get-tuple-element.26), channel_id=1, source_target_pairs={{0,2},{2,4},{4,6},{6,0},{1,3},{3,5},{5,7},{7,1},{8,10},{10,12},{12... | collective-permute-start | bytes 786440 | tf_op jit(solution)/shard_map/ppermute | solution.py:352
  17.9 14.3 %collective-permute-start.11 = (bf16[2,2,128,256]{3,2,1,0:T(8,128)(2,1)S(1)}, bf16[2,2,128,256]{3,2,1,0:T(8,128)(2,1)S(1)}, u32[]{:S(2)}, u32[]{:S(2)}) collective-permute-start(bf16[2,2,128,256]{3,2,1,0:T(8,128)(2,1)S(1)} %get-tuple-element.27), channel_id=1, source_target_pairs={{0,4},{2,6},{4,0},{6,2},{1,5},{3,7},{5,1},{7,3},{8,12},{10,14},{12... | collective-permute-start | bytes 786440 | tf_op jit(solution)/shard_map/ppermute | solution.py:352
  20.5 11.7 %collective-permute-start.12 = (bf16[2,2,128,256]{3,2,1,0:T(8,128)(2,1)S(1)}, bf16[2,2,128,256]{3,2,1,0:T(8,128)(2,1)S(1)}, u32[]{:S(2)}, u32[]{:S(2)}) collective-permute-start(bf16[2,2,128,256]{3,2,1,0:T(8,128)(2,1)S(1)} %get-tuple-element.28), channel_id=1, source_target_pairs={{0,6},{2,0},{4,2},{6,4},{1,7},{3,1},{5,3},{7,5},{8,14},{10,8},{12,... | collective-permute-start | bytes 786440 | tf_op jit(solution)/shard_map/ppermute | solution.py:352
  32.2 26.8 %collective-permute-start.17 = (bf16[2,8,128,256]{3,2,1,0:T(8,128)(2,1)S(1)}, bf16[2,8,128,256]{3,2,1,0:T(8,128)(2,1)S(1)}, u32[]{:S(2)}, u32[]{:S(2)}) collective-permute-start(bf16[2,8,128,256]{3,2,1,0:T(8,128)(2,1)S(1)} %join.1.refs_10_), channel_id=1, source_target_pairs={{0,56},{8,0},{16,8},{24,16},{32,24},{40,32},{48,40},{56,48},{1,57}... | collective-permute-start | bytes 3145736 | tf_op jit(solution)/shard_map/ppermute | solution.py:352
  35.3 27.0 %collective-permute-start.13 = (bf16[2,8,128,256]{3,2,1,0:T(8,128)(2,1)S(1)}, bf16[2,8,128,256]{3,2,1,0:T(8,128)(2,1)}, u32[]{:S(2)}, u32[]{:S(2)}) collective-permute-start(bf16[2,8,128,256]{3,2,1,0:T(8,128)(2,1)S(1)} %join.1.refs_10_), channel_id=1, source_target_pairs={{0,8},{8,16},{16,24},{24,32},{32,40},{40,48},{48,56},{56,0},{1,9},... | collective-permute-start | bytes 3145736 | tf_op jit(solution)/shard_map/ppermute | solution.py:352
  41.5 24.1 %collective-permute-start.4 = (bf16[8,512,128]{2,1,0:T(8,128)(2,1)S(1)}, bf16[8,512,128]{2,1,0:T(8,128)(2,1)S(1)}, u32[]{:S(2)}, u32[]{:S(2)}) collective-permute-start(bf16[8,512,128]{2,1,0:T(8,128)(2,1)S(1)} %all-to-all-done.refs_0_), channel_id=1, source_target_pairs={{0,6},{2,0},{4,2},{6,4},{1,7},{3,1},{5,3},{7,5},{8,14},{10,8},{12,... | collective-permute-start | bytes 3145736 | tf_op jit(solution)/shard_map/ppermute | solution.py:352
  44.1 25.0 %collective-permute-start.1 = (bf16[8,512,128]{2,1,0:T(8,128)(2,1)S(1)}, bf16[8,512,128]{2,1,0:T(8,128)(2,1)S(1)}, u32[]{:S(2)}, u32[]{:S(2)}) collective-permute-start(bf16[8,512,128]{2,1,0:T(8,128)(2,1)S(1)} %all-to-all-done.refs_0_), channel_id=1, source_target_pairs={{0,2},{2,4},{4,6},{6,0},{1,3},{3,5},{5,7},{7,1},{8,10},{10,12},{12... | collective-permute-start | bytes 3145736 | tf_op jit(solution)/shard_map/ppermute | solution.py:352
  59.0 24.6 %collective-permute-start.18 = (bf16[2,8,128,256]{3,2,1,0:T(8,128)(2,1)S(1)}, bf16[2,8,128,256]{3,2,1,0:T(8,128)(2,1)S(1)}, u32[]{:S(2)}, u32[]{:S(2)}) collective-permute-start(bf16[2,8,128,256]{3,2,1,0:T(8,128)(2,1)S(1)} %collective-permute-done.17.refs_12_), channel_id=1, source_target_pairs={{0,56},{8,0},{16,8},{24,16},{32,24},{40,32},{48,40},{56,48},{1,57}... | collective-permute-start | bytes 3145736 | tf_op jit(solution)/shard_map/ppermute | solution.py:352
  62.3 28.3 %collective-permute-start.14 = (bf16[2,8,128,256]{3,2,1,0:T(8,128)(2,1)}, bf16[2,8,128,256]{3,2,1,0:T(8,128)(2,1)S(1)}, u32[]{:S(2)}, u32[]{:S(2)}) collective-permute-start(bf16[2,8,128,256]{3,2,1,0:T(8,128)(2,1)} %collective-permute-done.13.refs_11_), channel_id=1, source_target_pairs={{0,8},{8,16},{16,24},{24,32},{32,40},{40,48},{48,56},{56,0},{1,9},... | collective-permute-start | bytes 3145736 | tf_op jit(solution)/shard_map/ppermute | solution.py:352
  65.6 25.5 %collective-permute-start.5 = (bf16[8,256,128]{2,1,0:T(8,128)(2,1)S(1)}, bf16[8,256,128]{2,1,0:T(8,128)(2,1)S(1)}, u32[]{:S(2)}, u32[]{:S(2)}) collective-permute-start(bf16[8,256,128]{2,1,0:T(8,128)(2,1)S(1)} %slice.21), channel_id=1, source_target_pairs={{0,6},{2,0},{4,2},{6,4},{1,7},{3,1},{5,3},{7,5},{8,14},{10,8},{12,... | collective-permute-start | bytes 1572872 | tf_op jit(solution)/shard_map/ppermute | solution.py:352
  83.7 21.7 %collective-permute-start.8 = (bf16[8,512,128]{2,1,0:T(8,128)(2,1)S(1)}, bf16[8,512,128]{2,1,0:T(8,128)(2,1)S(1)}, u32[]{:S(2)}, u32[]{:S(2)}) collective-permute-start(bf16[8,512,128]{2,1,0:T(8,128)(2,1)S(1)} %collective-permute-done.4.refs_8_), channel_id=1, source_target_pairs={{0,1},{1,0},{2,3},{3,2},{4,5},{5,4},{6,7},{7,6},{8,9},{9,8},{10,11... | collective-permute-start | bytes 3145736 | tf_op jit(solution)/shard_map/ppermute | solution.py:352
  85.7 26.0 %collective-permute-start.19 = (bf16[2,8,128,256]{3,2,1,0:T(8,128)(2,1)S(1)}, bf16[2,8,128,256]{3,2,1,0:T(8,128)(2,1)S(1)}, u32[]{:S(2)}, u32[]{:S(2)}) collective-permute-start(bf16[2,8,128,256]{3,2,1,0:T(8,128)(2,1)S(1)} %collective-permute-done.18.refs_14_), channel_id=1, source_target_pairs={{0,56},{8,0},{16,8},{24,16},{32,24},{40,32},{48,40},{56,48},{1,57}... | collective-permute-start | bytes 3145736 | tf_op jit(solution)/shard_map/ppermute | solution.py:352
  89.1 15.4 %collective-permute-start.3 = (bf16[8,256,128]{2,1,0:T(8,128)(2,1)S(1)}, bf16[8,256,128]{2,1,0:T(8,128)(2,1)S(1)}, u32[]{:S(2)}, u32[]{:S(2)}) collective-permute-start(bf16[8,256,128]{2,1,0:T(8,128)(2,1)S(1)} %slice.20), channel_id=1, source_target_pairs={{0,2},{2,4},{4,6},{6,0},{1,3},{3,5},{5,7},{7,1},{8,10},{10,12},{12... | collective-permute-start | bytes 1572872 | tf_op jit(solution)/shard_map/ppermute | solution.py:352
  90.6 21.9 %collective-permute-start.2 = (bf16[8,512,128]{2,1,0:T(8,128)(2,1)S(1)}, bf16[8,512,128]{2,1,0:T(8,128)(2,1)S(1)}, u32[]{:S(2)}, u32[]{:S(2)}) collective-permute-start(bf16[8,512,128]{2,1,0:T(8,128)(2,1)S(1)} %collective-permute-done.1.refs_2_), channel_id=1, source_target_pairs={{0,1},{1,0},{2,3},{3,2},{4,5},{5,4},{6,7},{7,6},{8,9},{9,8},{10,11... | collective-permute-start | bytes 3145736 | tf_op jit(solution)/shard_map/ppermute | solution.py:352
  91.1 25.7 %collective-permute-start.15 = (bf16[2,8,128,256]{3,2,1,0:T(8,128)(2,1)S(1)}, bf16[2,8,128,256]{3,2,1,0:T(8,128)(2,1)S(1)}, u32[]{:S(2)}, u32[]{:S(2)}) collective-permute-start(bf16[2,8,128,256]{3,2,1,0:T(8,128)(2,1)S(1)} %collective-permute-done.14.refs_13_), channel_id=1, source_target_pairs={{0,8},{8,16},{16,24},{24,32},{32,40},{40,48},{48,56},{56,0},{1,9},... | collective-permute-start | bytes 3145736 | tf_op jit(solution)/shard_map/ppermute | solution.py:352
  104.5 12.4 %collective-permute-start = (bf16[8,512,128]{2,1,0:T(8,128)(2,1)S(1)}, bf16[8,512,128]{2,1,0:T(8,128)(2,1)S(1)}, u32[]{:S(2)}, u32[]{:S(2)}) collective-permute-start(bf16[8,512,128]{2,1,0:T(8,128)(2,1)S(1)} %all-to-all-done.refs_0_), channel_id=1, source_target_pairs={{0,1},{1,0},{2,3},{3,2},{4,5},{5,4},{6,7},{7,6},{8,9},{9,8},{10,11... | collective-permute-start | bytes 3145736 | tf_op jit(solution)/shard_map/ppermute | solution.py:352
  105.3 11.7 %collective-permute-start.7 = (bf16[8,256,128]{2,1,0:T(8,128)(2,1)S(1)}, bf16[8,256,128]{2,1,0:T(8,128)(2,1)S(1)}, u32[]{:S(2)}, u32[]{:S(2)}) collective-permute-start(bf16[8,256,128]{2,1,0:T(8,128)(2,1)S(1)} %collective-permute-done.5.refs_5_), channel_id=1, source_target_pairs={{0,1},{1,0},{2,3},{3,2},{4,5},{5,4},{6,7},{7,6},{8,9},{9,8},{10,11... | collective-permute-start | bytes 1572872 | tf_op jit(solution)/shard_map/ppermute | solution.py:352
  111.7 5.3 %collective-permute-start.6 = (bf16[8,256,128]{2,1,0:T(8,128)(2,1)S(1)}, bf16[8,256,128]{2,1,0:T(8,128)(2,1)S(1)}, u32[]{:S(2)}, u32[]{:S(2)}) collective-permute-start(bf16[8,256,128]{2,1,0:T(8,128)(2,1)S(1)} %collective-permute-done.3.refs_4_), channel_id=1, source_target_pairs={{0,1},{1,0},{2,3},{3,2},{4,5},{5,4},{6,7},{7,6},{8,9},{9,8},{10,11... | collective-permute-start | bytes 1572872 | tf_op jit(solution)/shard_map/ppermute | solution.py:352
  112.5 15.1 %collective-permute-start.20 = (bf16[8,128,256]{2,1,0:T(8,128)(2,1)S(1)}, bf16[8,128,256]{2,1,0:T(8,128)(2,1)S(1)}, u32[]{:S(2)}, u32[]{:S(2)}) collective-permute-start(bf16[8,128,256]{2,1,0:T(8,128)(2,1)S(1)} %slice_bitcast_fusion), channel_id=1, source_target_pairs={{0,56},{8,0},{16,8},{24,16},{32,24},{40,32},{48,40},{56,48},{1,57}... | collective-permute-start | bytes 1572872 | tf_op jit(solution)/shard_map/ppermute | solution.py:352
  116.9 13.6 %collective-permute-start.16 = (bf16[8,128,256]{2,1,0:T(8,128)(2,1)S(1)}, bf16[8,128,256]{2,1,0:T(8,128)(2,1)S(1)}, u32[]{:S(2)}, u32[]{:S(2)}) collective-permute-start(bf16[8,128,256]{2,1,0:T(8,128)(2,1)S(1)} %slice_bitcast_fusion.1), channel_id=1, source_target_pairs={{0,8},{8,16},{16,24},{24,32},{32,40},{40,48},{48,56},{56,0},{1,9},... | collective-permute-start | bytes 1572872 | tf_op jit(solution)/shard_map/ppermute | solution.py:352
  161.8 9.6 %collective-permute-start.21 = (f32[128,512]{1,0:T(8,128)S(1)}, f32[128,512]{1,0:T(8,128)S(1)}, u32[]{:S(2)}, u32[]{:S(2)}) collective-permute-start(f32[128,512]{1,0:T(8,128)S(1)} %get-tuple-element.35), channel_id=1, source_target_pairs={{0,128},{64,192},{128,0},{192,64},{1,129},{65,193},{129,1},{193,65... | collective-permute-start | bytes 786440 | tf_op jit(solution)/shard_map/ppermute | solution.py:352
  165.4 12.4 %collective-permute-start.22 = (f32[128,512]{1,0:T(8,128)S(1)}, f32[128,512]{1,0:T(8,128)S(1)}, u32[]{:S(2)}, u32[]{:S(2)}) collective-permute-start(f32[128,512]{1,0:T(8,128)S(1)} %get-tuple-element.36), channel_id=1, source_target_pairs={{0,64},{64,128},{128,192},{192,0},{1,65},{65,129},{129,193},{193,1... | collective-permute-start | bytes 786440 | tf_op jit(solution)/shard_map/ppermute | solution.py:352
  165.4 12.4 %collective-permute-start.23 = (f32[128,512]{1,0:T(8,128)S(1)}, f32[128,512]{1,0:T(8,128)S(1)}, u32[]{:S(2)}, u32[]{:S(2)}) collective-permute-start(f32[128,512]{1,0:T(8,128)S(1)} %get-tuple-element.37), channel_id=1, source_target_pairs={{0,192},{64,0},{128,64},{192,128},{1,193},{65,1},{129,65},{193,129... | collective-permute-start | bytes 786440 | tf_op jit(solution)/shard_map/ppermute | solution.py:352
  (19 other events, 454.9 us)

commit v2 on v1

--- a/solution.py
+++ b/solution.py
@@ -16,6 +16,8 @@
 WIDE = TILE // 2
 LANES = 128
 MEMBERS = NZ * BLOCKS
+PARTS = 2 * BLOCKS
+CUT = 7
 SEQ = ("z", "y", "core")
 F32, BF16 = jnp.float32, jnp.bfloat16
 MIB = 1 << 20
@@ -147,7 +149,7 @@
 def join_kernel(*refs):
     for h in range(2):
         for k in range(NY):
-            refs[NY][h, k * NC : (k + 1) * NC] = refs[k][h]
+            refs[NY][pl.ds(h * BLOCKS + k * NC, NC)] = refs[k][h]
 
 
 def join(pairs):
@@ -155,7 +157,7 @@
         join_kernel,
         in_specs=[VMEM] * NY,
         out_specs=VMEM,
-        out_shape=jax.ShapeDtypeStruct((2, BLOCKS, TOK, WIDE), BF16),
+        out_shape=jax.ShapeDtypeStruct((PARTS, TOK, WIDE), BF16),
         compiler_params=params(8),
         cost_estimate=cost(0, 2 * MIB),
         name="join",
@@ -184,34 +186,45 @@
     ]
 
 
+def part_of(parts, h, b):
+    i = h * BLOCKS + b
+    if len(parts) == 1:
+        return parts[0][i]
+    return parts[0][i] if i < CUT else parts[1][i - CUT]
+
+
 def side_by_side(buf):
     return jnp.concatenate([buf[b] for b in range(BLOCKS)], axis=1)
 
 
-def norm_kernel(chunks, has_acc, is_last, z_ref, doc_ref, *refs):
+def norm_kernel(chunks, is_last, z_ref, doc_ref, *refs):
     n = len(chunks)
-    acts, refs = refs[:ACTS], refs[ACTS:]
     many = 2 if is_last else n
+    if is_last:
+        late_ref, refs = refs[0], refs[1:]
+    else:
+        acts, refs = refs[:ACTS], refs[ACTS:]
     grads, refs = refs[:many], refs[many:]
-    if has_acc and not is_last:
-        refs = refs[1:]
     acc_ref, refs = refs[0], refs[1:]
     if is_last:
-        out_ref, refs = refs[0], refs[1:]
-        acts_buf, sem = refs
+        (out_ref,) = refs
     else:
-        acts_buf, grads_buf, sem = refs
+        late_ref, acts_buf, grads_buf, sem = refs
     copies = []
     for i, s in enumerate(chunks):
-        copies.append(acts_copies(acts, z_ref[s], acts_buf.at[i], sem.at[i]))
+        copies.append([])
         if not is_last:
+            copies[-1] += acts_copies(acts, z_ref[s], acts_buf.at[i], sem.at[i])
             copies[-1].append(
                 pltpu.make_async_copy(grads[i], grads_buf.at[i], sem.at[i, ACTS])
             )
     for several in copies:
         for copy in several:
             copy.start()
-    if not has_acc:
+    if not is_last:
+        late_copies = acts_copies(acts, z_ref[NZ - 1], late_ref, sem.at[n])
+        for copy in late_copies:
+            copy.start()
         acc_ref[...] = jnp.zeros_like(acc_ref)
     for i, s in enumerate(chunks):
         for copy in copies[i]:
@@ -221,18 +234,21 @@
 
             @pl.when(functools.reduce(jnp.logical_or, held))
             def _():
-                x = side_by_side(acts_buf.at[i])
+                x = side_by_side(late_ref if is_last else acts_buf.at[i])
                 for h in range(2):
-                    g = grads[h] if is_last else grads_buf.at[i, h]
+                    parts = grads if is_last else (grads_buf.at[i],)
                     kept = [
-                        jnp.where(held[b], g[b], jnp.zeros((TOK, WIDE), BF16))
+                        jnp.where(held[b], part_of(parts, h, b), jnp.zeros((TOK, WIDE), BF16))
                         for b in range(BLOCKS)
                     ]
                     acc_ref[d, :, h * WIDE : (h + 1) * WIDE] += jnp.dot(
                         x, jnp.concatenate(kept, axis=0), preferred_element_type=F32
                     )
 
-    if is_last:
+    if not is_last:
+        for copy in late_copies:
+            copy.wait()
+    else:
         lane = lax.broadcasted_iota(jnp.int32, (1, LANES), 1)
         row = jnp.zeros((1, LANES), F32)
         for d in range(DOCS):
@@ -241,31 +257,32 @@
         out_ref[...] = jnp.broadcast_to(row[None], out_ref.shape)
 
 
-def norm_call(chunks, z_list, docs, acts, grads, acc=None, is_last=False):
+def norm_call(chunks, z_list, docs, acts, grads, sums=None):
     n = len(chunks)
-    operands = [z_list, docs, *map(in_hbm, acts)]
-    for s in chunks:
-        operands += grads[s] if is_last else [in_hbm(grads[s])]
-    in_specs = [SMEM] * 2 + [ANY] * ACTS + ([VMEM] * 2 if is_last else [ANY] * n)
-    aliases = {}
-    if acc is not None:
-        operands.append(acc)
-        in_specs.append(VMEM)
-        if not is_last:
-            aliases = {len(operands) - 1: 0}
-    scratch = [pltpu.VMEM((n, BLOCKS, TILE, TOK), BF16)]
+    is_last = sums is not None
+    operands = [z_list, docs]
     if is_last:
+        acc, late = sums
+        operands += [late, *grads[chunks[0]], acc]
         out_shape = jax.ShapeDtypeStruct((MEMBERS, 1, LANES), F32)
+        scratch = []
     else:
-        out_shape = jax.ShapeDtypeStruct((DOCS, TILE, TILE), F32)
-        scratch.append(pltpu.VMEM((n, 2, BLOCKS, TOK, WIDE), BF16))
-    return pl.pallas_call(
-        functools.partial(norm_kernel, chunks, acc is not None, is_last),
-        in_specs=in_specs,
-        out_specs=VMEM,
+        operands += map(in_hbm, [*acts, *(grads[s] for s in chunks)])
+        out_shape = [
+            jax.ShapeDtypeStruct((DOCS, TILE, TILE), F32),
+            jax.ShapeDtypeStruct((BLOCKS, TILE, TOK), BF16),
+        ]
+        scratch = [
+            pltpu.VMEM((n, BLOCKS, TILE, TOK), BF16),
+            pltpu.VMEM((n, PARTS, TOK, WIDE), BF16),
+            pltpu.SemaphoreType.DMA((n + 1, ACTS + 2)),
+        ]
+    return pl.pallas_call(
+        functools.partial(norm_kernel, chunks, is_last),
+        in_specs=[SMEM] * 2 + [VMEM if is_last else ANY] * (len(operands) - 2),
+        out_specs=VMEM if is_last else [VMEM] * 2,
         out_shape=out_shape,
-        input_output_aliases=aliases,
-        scratch_shapes=scratch + [pltpu.SemaphoreType.DMA((n, ACTS + 2))],
+        scratch_shapes=scratch,
         compiler_params=params(12 + 2 * n),
         cost_estimate=cost(2 * n * CHUNK * TILE * TILE, 3 * n * MIB),
         name="norm_" + "_".join(str(s) for s in chunks),
@@ -274,19 +291,13 @@
 
 def grad_kernel(z_ref, doc_ref, norm_ref, *refs):
     acts, refs = refs[:ACTS], refs[ACTS:]
-    grads, refs = refs[: NZ + 1], refs[NZ + 1 :]
+    grads, refs = refs[: NZ - 1], refs[NZ - 1 :]
+    late_acts, late_grads, refs = refs[0], refs[1:3], refs[3:]
     outs, ratio_ref, acc_ref, acts_buf, grads_buf, sem = refs[:4], *refs[4:]
     copies = []
-    for s in range(NZ):
-        if s < NZ - 1:
-            pieces = [(grads[s], grads_buf.at[s])]
-        else:
-            pieces = [(grads[s + h], grads_buf.at[s, h]) for h in range(2)]
+    for s in range(NZ - 1):
         copies.append(
-            [
-                pltpu.make_async_copy(src, dst, sem.at[s, ACTS + i])
-                for i, (src, dst) in enumerate(pieces)
-            ]
+            [pltpu.make_async_copy(grads[s], grads_buf.at[s], sem.at[s, ACTS])]
             + acts_copies(acts, z_ref[s], acts_buf.at[s], sem.at[s])
         )
         for copy in copies[s]:
@@ -298,22 +309,25 @@
     ratio_ref[...] = doc_norm / threshold
     factor = 1.0 / jnp.maximum(doc_norm, threshold)
     clip = [jnp.sum(jnp.where(lane == d, factor, 0)) for d in range(DOCS)]
-    for s in range(NZ):
-        for copy in copies[s]:
-            copy.wait()
+    for s in (NZ - 1, *range(NZ - 1)):
+        if s < NZ - 1:
+            for copy in copies[s]:
+                copy.wait()
+        parts = (grads_buf.at[s],) if s < NZ - 1 else late_grads
+        x = side_by_side(acts_buf.at[s] if s < NZ - 1 else late_acts)
         for h in range(2):
             scaled = []
             for b in range(BLOCKS):
                 doc = doc_ref[s * BLOCKS + b]
                 mine = jnp.where(doc == 0, clip[0], jnp.where(doc == 1, clip[1], clip[2]))
-                scaled.append((mine * grads_buf[s, h, b].astype(F32)).astype(BF16))
+                scaled.append((mine * part_of(parts, h, b).astype(F32)).astype(BF16))
             product = jnp.dot(
-                side_by_side(acts_buf.at[s]),
+                x,
                 jnp.concatenate(scaled, axis=0),
                 preferred_element_type=F32,
             )
             cols = slice(h * WIDE, (h + 1) * WIDE)
-            if s == 0:
+            if s == NZ - 1:
                 acc_ref[:, cols] = product
             else:
                 acc_ref[:, cols] += product
@@ -323,20 +337,21 @@
         outs[k][...] = acc_ref[pl.ds(first, TOK), :]
 
 
-def grad_call(z_list, docs, norms, acts, grads):
+def grad_call(z_list, docs, norms, acts, grads, late):
     operands = [z_list, docs, norms, *map(in_hbm, acts)]
-    operands += map(in_hbm, [*grads[:-1], *grads[-1]])
+    operands += map(in_hbm, grads[:-1])
+    operands += [late, *grads[-1]]
     return pl.pallas_call(
         grad_kernel,
-        in_specs=[SMEM] * 2 + [VMEM] + [ANY] * (ACTS + NZ + 1),
+        in_specs=[SMEM] * 2 + [VMEM] + [ANY] * (ACTS + NZ - 1) + [VMEM] * 3,
         out_specs=[VMEM] * 5,
         out_shape=[jax.ShapeDtypeStruct((TOK, TILE), F32)] * 4
         + [jax.ShapeDtypeStruct((1, LANES), F32)],
         scratch_shapes=[
             pltpu.VMEM((TILE, TILE), F32),
-            pltpu.VMEM((NZ, BLOCKS, TILE, TOK), BF16),
-            pltpu.VMEM((NZ, 2, BLOCKS, TOK, WIDE), BF16),
-            pltpu.SemaphoreType.DMA((NZ, ACTS + 2)),
+            pltpu.VMEM((NZ - 1, BLOCKS, TILE, TOK), BF16),
+            pltpu.VMEM((NZ - 1, PARTS, TOK, WIDE), BF16),
+            pltpu.SemaphoreType.DMA((NZ - 1, ACTS + 1)),
         ],
         compiler_params=params(32),
         cost_estimate=cost(2 * NZ * CHUNK * TILE * TILE, 18 * MIB),
@@ -371,16 +386,16 @@
     far = [move(right[:, :WIDE], "y", 1), move(left[:, WIDE:], "y", -1)]
     right_c, left_c = move(right, "core", 1), move(left, "core", 1)
     last = [
-        move(after(g[-3][0], *far, right_c, left_c), "z", 1),
-        move(after(g[3][1], *far, right_c, left_c), "z", -1),
+        move(after(g[-3][:CUT], *far, right_c, left_c), "z", 1),
+        move(after(g[3][CUT:], *far, right_c, left_c), "z", -1),
     ]
     acts = [own, own_c, right, right_c, *far, *(move(x, "core", 1) for x in far), left, left_c]
     chunks = [g[s] for s in STEPS[:-1]] + [last]
-    acc = norm_call((0, 1, 2, 3, 4, 5, 6), z_list, docs, acts, chunks)
-    partial = norm_call((7,), z_list, docs, acts, chunks, acc, is_last=True)
+    sums = norm_call((0, 1, 2, 3, 4, 5, 6), z_list, docs, acts, chunks)
+    partial = norm_call((7,), z_list, docs, acts, chunks, sums)
     norms = lax.all_to_all(partial, SEQ, split_axis=0, concat_axis=0, tiled=True)
 
-    *parts, ratio = grad_call(z_list, docs, norms, acts, chunks)
+    *parts, ratio = grad_call(z_list, docs, norms, acts, chunks, sums[1])
     total = parts[0]
     for k in (2, 1, 3):
         total = total + move(parts[k], "dp", k)

time: 179 us -> 175 us (0.978)
  starting transfers between devices: 46.4 us -> 43.1 us
    ppermute x24, starting transfers between devices: 37.4 us -> 34 us  [move(): return lax.ppermute(x, axis, ring(lax.axis_size(axis), k))]
  transfers between devices with their start and end apart: 25 -> 25, of which waited for: 13 -> 11; matrix products, arithmetic and copies ran while one was open for 0% -> 0% of each run, Pallas kernels for 6% -> 7%
where the time goes in v2:
time: 175 us
  waiting for transfers between devices  84.9 us (49%)
  starting transfers between devices  43.1 us (25%)
  Pallas kernels  23.7 us (14%)
  blocking collectives  20.4 us (12%)
    ppermute x24, waiting for transfers between devices, move(): return lax.ppermute(x, axis, ring(lax.axis_size(axis), k))  78.6 us
    ppermute x24, starting transfers between devices, move(): return lax.ppermute(x, axis, ring(lax.axis_size(axis), k))  34 us
    all_to_all x1, blocking collectives, body(): lax.all_to_all(partial, SEQ, split_axis=0, concat_axis=0, tiled=True)  20.4 us
    pallas_call x2, Pallas kernels, norm_call(): pl.pallas_call(functools.partial(norm_kernel, chunks, is_last), in_specs=...  11.7 us
    all_to_all x1, starting transfers between devices, body(): own = lax.all_to_all(acts_t, 'z', split_axis=0, concat_axis=0, tiled=True)  9.03 us
    pallas_call x1, Pallas kernels, grad_call(): pl.pallas_call(grad_kernel, in_specs=[SMEM] * 2 + [VMEM] + [ANY] * (ACTS...  7.67 us
    all_to_all x1, waiting for transfers between devices, body(): own = lax.all_to_all(acts_t, 'z', split_axis=0, concat_axis=0, tiled=True)  6.24 us
  transfers between devices with their start and end apart: 25, of which 11 were waited for; matrix products, arithmetic and copies ran while one was open for 0% of the time, Pallas kernels for 7%

profile of v2, /device:TPU:1, one launch (start us, length us, event | category | flops | bytes accessed | tf_op | source)
XLA Modules:
  0.0 175.3 jit_solution(7808515706538052217)
XLA Ops:
  0.6 2.8 %open_acts.1 = (bf16[8,512,128]{2,1,0:T(8,128)(2,1)}, s32[8]{0:T(128)S(1)}, s32[64]{0:T(128)S(1)}) custom-call(bf16[128,4096]{1,0:T(8,128)(2,1)} %acts_ref.1, s32[1,3]{1,0:T(1,128)} %units_in.1), custom_call_target="tpu_custom_call" | custom-call | bytes 2097152 | tf_op jit(solution)/shard_map/open_acts/pallas_call | solution.py:78
  3.4 9.0 %all-to-all-start = ((bf16[8,512,128]{2,1,0:T(8,128)(2,1)}), bf16[8,512,128]{2,1,0:T(8,128)(2,1)S(1)}, u32[]{:S(2)}, u32[]{:S(2)}) async-start(bf16[8,512,128]{2,1,0:T(8,128)(2,1)} %get-tuple-element.24), calls=%async_computation | async-start | bytes 2097152 | tf_op jit(solution)/shard_map/all_to_all | solution.py:377
  17.9 2.6 %collective-permute-start.11 = (bf16[2,2,128,256]{3,2,1,0:T(8,128)(2,1)S(1)}, bf16[2,2,128,256]{3,2,1,0:T(8,128)(2,1)S(1)}, u32[]{:S(2)}, u32[]{:S(2)}) collective-permute-start(bf16[2,2,128,256]{3,2,1,0:T(8,128)(2,1)S(1)} %get-tuple-element.29), channel_id=1, source_target_pairs={{0,4},{2,6},{4,0},{6,2},{1,5},{3,7},{5,1},{7,3},{8,12},{10,14},{12... | collective-permute-start | bytes 786440 | tf_op jit(solution)/shard_map/ppermute | solution.py:367
  21.6 3.9 %collective-permute-done.10.refs_1_ = bf16[2,2,128,256]{3,2,1,0:T(8,128)(2,1)S(1)} collective-permute-done((bf16[2,2,128,256]{3,2,1,0:T(8,128)(2,1)S(1)}, bf16[2,2,128,256]{3,2,1,0:T(8,128)(2,1)S(1)}, u32[]{:S(2)}, u32[]{:S(2)}) %collective-permute-start.10) | collective-permute-done | bytes 262176 | tf_op jit(solution)/shard_map/ppermute | solution.py:367
  25.4 6.7 %collective-permute-done.11.refs_2_ = bf16[2,2,128,256]{3,2,1,0:T(8,128)(2,1)S(1)} collective-permute-done((bf16[2,2,128,256]{3,2,1,0:T(8,128)(2,1)S(1)}, bf16[2,2,128,256]{3,2,1,0:T(8,128)(2,1)S(1)}, u32[]{:S(2)}, u32[]{:S(2)}) %collective-permute-start.11) | collective-permute-done | bytes 262176 | tf_op jit(solution)/shard_map/ppermute | solution.py:367
  32.2 3.0 %collective-permute-start.14 = (bf16[16,128,256]{2,1,0:T(8,128)(2,1)S(1)}, bf16[16,128,256]{2,1,0:T(8,128)(2,1)S(1)}, u32[]{:S(2)}, u32[]{:S(2)}) collective-permute-start(bf16[16,128,256]{2,1,0:T(8,128)(2,1)S(1)} %join.1.refs_10_), channel_id=1, source_target_pairs={{0,56},{8,0},{16,8},{24,16},{32,24},{40,32},{48,40},{56,48},{1,57}... | collective-permute-start | bytes 3145736 | tf_op jit(solution)/shard_map/ppermute | solution.py:367
  35.3 6.2 %all-to-all-done.refs_0_ = bf16[8,512,128]{2,1,0:T(8,128)(2,1)S(1)} async-done(((bf16[8,512,128]{2,1,0:T(8,128)(2,1)}), bf16[8,512,128]{2,1,0:T(8,128)(2,1)S(1)}, u32[]{:S(2)}, u32[]{:S(2)}) %all-to-all-start) | async-done | bytes 1048608 | tf_op jit(solution)/shard_map/all_to_all | solution.py:377
  41.5 2.6 %collective-permute-start.4 = (bf16[8,512,128]{2,1,0:T(8,128)(2,1)S(1)}, bf16[8,512,128]{2,1,0:T(8,128)(2,1)S(1)}, u32[]{:S(2)}, u32[]{:S(2)}) collective-permute-start(bf16[8,512,128]{2,1,0:T(8,128)(2,1)S(1)} %all-to-all-done.refs_0_), channel_id=1, source_target_pairs={{0,6},{2,0},{4,2},{6,4},{1,7},{3,1},{5,3},{7,5},{8,14},{10,8},{12,... | collective-permute-start | bytes 3145736 | tf_op jit(solution)/shard_map/ppermute | solution.py:367
  44.1 14.9 %collective-permute-done.14.refs_12_ = bf16[16,128,256]{2,1,0:T(8,128)(2,1)S(1)} collective-permute-done((bf16[16,128,256]{2,1,0:T(8,128)(2,1)S(1)}, bf16[16,128,256]{2,1,0:T(8,128)(2,1)S(1)}, u32[]{:S(2)}, u32[]{:S(2)}) %collective-permute-start.14) | collective-permute-done | bytes 1048608 | tf_op jit(solution)/shard_map/ppermute | solution.py:367
  59.1 3.3 %collective-permute-start.16 = (bf16[16,128,256]{2,1,0:T(8,128)(2,1)S(1)}, bf16[16,128,256]{2,1,0:T(8,128)(2,1)S(1)}, u32[]{:S(2)}, u32[]{:S(2)}) collective-permute-start(bf16[16,128,256]{2,1,0:T(8,128)(2,1)S(1)} %collective-permute-done.14.refs_12_), channel_id=1, source_target_pairs={{0,56},{8,0},{16,8},{24,16},{32,24},{40,32},{48,40},{56,48},{1,57}... | collective-permute-start | bytes 3145736 | tf_op jit(solution)/shard_map/ppermute | solution.py:367
  62.3 3.3 %collective-permute-done.4.refs_8_ = bf16[8,512,128]{2,1,0:T(8,128)(2,1)S(1)} collective-permute-done((bf16[8,512,128]{2,1,0:T(8,128)(2,1)S(1)}, bf16[8,512,128]{2,1,0:T(8,128)(2,1)S(1)}, u32[]{:S(2)}, u32[]{:S(2)}) %collective-permute-start.4) | collective-permute-done | bytes 1048608 | tf_op jit(solution)/shard_map/ppermute | solution.py:367
  65.6 3.5 %collective-permute-start.5 = (bf16[8,256,128]{2,1,0:T(8,128)(2,1)S(1)}, bf16[8,256,128]{2,1,0:T(8,128)(2,1)S(1)}, u32[]{:S(2)}, u32[]{:S(2)}) collective-permute-start(bf16[8,256,128]{2,1,0:T(8,128)(2,1)S(1)} %slice.21), channel_id=1, source_target_pairs={{0,6},{2,0},{4,2},{6,4},{1,7},{3,1},{5,3},{7,5},{8,14},{10,8},{12,... | collective-permute-start | bytes 1572872 | tf_op jit(solution)/shard_map/ppermute | solution.py:367
  69.2 14.4 %collective-permute-done.16.refs_14_ = bf16[16,128,256]{2,1,0:T(8,128)(2,1)S(1)} collective-permute-done((bf16[16,128,256]{2,1,0:T(8,128)(2,1)S(1)}, bf16[16,128,256]{2,1,0:T(8,128)(2,1)S(1)}, u32[]{:S(2)}, u32[]{:S(2)}) %collective-permute-start.16) | collective-permute-done | bytes 1048608 | tf_op jit(solution)/shard_map/ppermute | solution.py:367
  83.7 2.0 %collective-permute-start.8 = (bf16[8,512,128]{2,1,0:T(8,128)(2,1)S(1)}, bf16[8,512,128]{2,1,0:T(8,128)(2,1)S(1)}, u32[]{:S(2)}, u32[]{:S(2)}) collective-permute-start(bf16[8,512,128]{2,1,0:T(8,128)(2,1)S(1)} %collective-permute-done.4.refs_8_), channel_id=1, source_target_pairs={{0,1},{1,0},{2,3},{3,2},{4,5},{5,4},{6,7},{7,6},{8,9},{9,8},{10,11... | collective-permute-start | bytes 3145736 | tf_op jit(solution)/shard_map/ppermute | solution.py:367
  85.7 3.4 %collective-permute-start.18 = (bf16[16,128,256]{2,1,0:T(8,128)(2,1)S(1)}, bf16[16,128,256]{2,1,0:T(8,128)(2,1)S(1)}, u32[]{:S(2)}, u32[]{:S(2)}) collective-permute-start(bf16[16,128,256]{2,1,0:T(8,128)(2,1)S(1)} %collective-permute-done.16.refs_14_), channel_id=1, source_target_pairs={{0,56},{8,0},{16,8},{24,16},{32,24},{40,32},{48,40},{56,48},{1,57}... | collective-permute-start | bytes 3145736 | tf_op jit(solution)/shard_map/ppermute | solution.py:367
  90.0 21.7 %collective-permute-done.18.refs_16_ = bf16[16,128,256]{2,1,0:T(8,128)(2,1)S(1)} collective-permute-done((bf16[16,128,256]{2,1,0:T(8,128)(2,1)S(1)}, bf16[16,128,256]{2,1,0:T(8,128)(2,1)S(1)}, u32[]{:S(2)}, u32[]{:S(2)}) %collective-permute-start.18) | collective-permute-done | bytes 1048608 | tf_op jit(solution)/shard_map/ppermute | solution.py:367
  112.5 3.5 %collective-permute-start.20 = (bf16[9,128,256]{2,1,0:T(8,128)(2,1)S(1)}, bf16[9,128,256]{2,1,0:T(8,128)(2,1)S(1)}, u32[]{:S(2)}, u32[]{:S(2)}) collective-permute-start(bf16[9,128,256]{2,1,0:T(8,128)(2,1)S(1)} %slice.23), channel_id=1, source_target_pairs={{0,56},{8,0},{16,8},{24,16},{32,24},{40,32},{48,40},{56,48},{1,57}... | collective-permute-start | bytes 1769480 | tf_op jit(solution)/shard_map/ppermute | solution.py:367
  117.7 10.0 %norm_0_1_2_3_4_5_6.1 = (f32[3,512,512]{2,1,0:T(8,128)S(1)}, bf16[8,512,128]{2,1,0:T(8,128)(2,1)S(1)}) custom-call(s32[8]{0:T(128)S(1)} %get-tuple-element.22.z_ref, s32[64]{0:T(128)S(1)} %get-tuple-element.23.doc_ref, bf16[8,512,128]{2,1,0:T(8,128)(2,1)} %copy-done.1, bf16[8,512,128]{2,1,0:T(8,128)(2,1)} %copy-done.11, bf16[8,512,128]{2,1,0:T(8,128)(2,1)} %copy-done.4, ...), custom_call_target="tpu_custom_call" | custom-call | flops 3758096384 | bytes 22020096 | tf_op jit(solution)/shard_map/norm_0_1_2_3_4_5_6/pallas_call | solution.py:280
  131.0 20.4 %all_to_all.10.norm_ref = f32[64,1,128]{2,1,0:T(1,128)S(1)} all-to-all(f32[64,1,128]{2,1,0:T(1,128)S(1)} %norm_7.1), channel_id=1, replica_groups=mesh['dp'=4,'z'=8,'y'=4,'core'=2] {'z','y','core'}, dimensions={0} | all-to-all | bytes 65536 | tf_op jit(solution)/shard_map/all_to_all | solution.py:396
  151.3 7.7 %grad.1 = (f32[128,512]{1,0:T(8,128)S(1)}, f32[128,512]{1,0:T(8,128)S(1)}, f32[128,512]{1,0:T(8,128)S(1)}, f32[128,512]{1,0:T(8,128)S(1)}, f32[1,128]{1,0:T(1,128)}) custom-call(s32[8]{0:T(128)S(1)} %get-tuple-element.22.z_ref, s32[64]{0:T(128)S(1)} %get-tuple-element.23.doc_ref, f32[64,1,128]{2,1,0:T(1,128)S(1)} %all_to_all.10.norm_ref, ...), custom_call_target="tpu_custom_call" | custom-call | flops 4294967296 | bytes 18874368 | tf_op jit(solution)/shard_map/grad/pallas_call | solution.py:344
  159.0 2.1 %collective-permute-start.21 = (f32[128,512]{1,0:T(8,128)S(1)}, f32[128,512]{1,0:T(8,128)S(1)}, u32[]{:S(2)}, u32[]{:S(2)}) collective-permute-start(f32[128,512]{1,0:T(8,128)S(1)} %get-tuple-element.39), channel_id=1, source_target_pairs={{0,128},{64,192},{128,0},{192,64},{1,129},{65,193},{129,1},{193,65... | collective-permute-start | bytes 786440 | tf_op jit(solution)/shard_map/ppermute | solution.py:367
  161.9 2.0 %collective-permute-start.23 = (f32[128,512]{1,0:T(8,128)S(1)}, f32[128,512]{1,0:T(8,128)S(1)}, u32[]{:S(2)}, u32[]{:S(2)}) collective-permute-start(f32[128,512]{1,0:T(8,128)S(1)} %get-tuple-element.41), channel_id=1, source_target_pairs={{0,192},{64,0},{128,64},{192,128},{1,193},{65,1},{129,65},{193,129... | collective-permute-start | bytes 786440 | tf_op jit(solution)/shard_map/ppermute | solution.py:367
  163.8 4.0 %collective-permute-done.21 = f32[128,512]{1,0:T(8,128)S(1)} collective-permute-done((f32[128,512]{1,0:T(8,128)S(1)}, f32[128,512]{1,0:T(8,128)S(1)}, u32[]{:S(2)}, u32[]{:S(2)}) %collective-permute-start.21) | collective-permute-done | bytes 262176 | tf_op jit(solution)/shard_map/ppermute | solution.py:367
  167.8 6.6 %collective-permute-done.22 = f32[128,512]{1,0:T(8,128)S(1)} collective-permute-done((f32[128,512]{1,0:T(8,128)S(1)}, f32[128,512]{1,0:T(8,128)S(1)}, u32[]{:S(2)}, u32[]{:S(2)}) %collective-permute-start.22) | collective-permute-done | bytes 262176 | tf_op jit(solution)/shard_map/ppermute | solution.py:367
  (71 shorter events, 14.8 us)
Async XLA Ops:
  3.4 38.1 %all-to-all-start = ((bf16[8,512,128]{2,1,0:T(8,128)(2,1)}), bf16[8,512,128]{2,1,0:T(8,128)(2,1)S(1)}, u32[]{:S(2)}, u32[]{:S(2)}) async-start(bf16[8,512,128]{2,1,0:T(8,128)(2,1)} %get-tuple-element.24), calls=%async_computation | async-start | bytes 2097152 | tf_op jit(solution)/shard_map/all_to_all | solution.py:377
  16.5 8.9 %collective-permute-start.10 = (bf16[2,2,128,256]{3,2,1,0:T(8,128)(2,1)S(1)}, bf16[2,2,128,256]{3,2,1,0:T(8,128)(2,1)S(1)}, u32[]{:S(2)}, u32[]{:S(2)}) collective-permute-start(bf16[2,2,128,256]{3,2,1,0:T(8,128)(2,1)S(1)} %get-tuple-element.28), channel_id=1, source_target_pairs={{0,2},{2,4},{4,6},{6,0},{1,3},{3,5},{5,7},{7,1},{8,10},{10,12},{12... | collective-permute-start | bytes 786440 | tf_op jit(solution)/shard_map/ppermute | solution.py:367
  17.9 14.3 %collective-permute-start.11 = (bf16[2,2,128,256]{3,2,1,0:T(8,128)(2,1)S(1)}, bf16[2,2,128,256]{3,2,1,0:T(8,128)(2,1)S(1)}, u32[]{:S(2)}, u32[]{:S(2)}) collective-permute-start(bf16[2,2,128,256]{3,2,1,0:T(8,128)(2,1)S(1)} %get-tuple-element.29), channel_id=1, source_target_pairs={{0,4},{2,6},{4,0},{6,2},{1,5},{3,7},{5,1},{7,3},{8,12},{10,14},{12... | collective-permute-start | bytes 786440 | tf_op jit(solution)/shard_map/ppermute | solution.py:367
  20.5 11.7 %collective-permute-start.12 = (bf16[2,2,128,256]{3,2,1,0:T(8,128)(2,1)S(1)}, bf16[2,2,128,256]{3,2,1,0:T(8,128)(2,1)S(1)}, u32[]{:S(2)}, u32[]{:S(2)}) collective-permute-start(bf16[2,2,128,256]{3,2,1,0:T(8,128)(2,1)S(1)} %get-tuple-element.30), channel_id=1, source_target_pairs={{0,6},{2,0},{4,2},{6,4},{1,7},{3,1},{5,3},{7,5},{8,14},{10,8},{12,... | collective-permute-start | bytes 786440 | tf_op jit(solution)/shard_map/ppermute | solution.py:367
  32.2 26.8 %collective-permute-start.14 = (bf16[16,128,256]{2,1,0:T(8,128)(2,1)S(1)}, bf16[16,128,256]{2,1,0:T(8,128)(2,1)S(1)}, u32[]{:S(2)}, u32[]{:S(2)}) collective-permute-start(bf16[16,128,256]{2,1,0:T(8,128)(2,1)S(1)} %join.1.refs_10_), channel_id=1, source_target_pairs={{0,56},{8,0},{16,8},{24,16},{32,24},{40,32},{48,40},{56,48},{1,57}... | collective-permute-start | bytes 3145736 | tf_op jit(solution)/shard_map/ppermute | solution.py:367
  35.3 27.0 %collective-permute-start.13 = (bf16[16,128,256]{2,1,0:T(8,128)(2,1)S(1)}, bf16[16,128,256]{2,1,0:T(8,128)(2,1)}, u32[]{:S(2)}, u32[]{:S(2)}) collective-permute-start(bf16[16,128,256]{2,1,0:T(8,128)(2,1)S(1)} %join.1.refs_10_), channel_id=1, source_target_pairs={{0,8},{8,16},{16,24},{24,32},{32,40},{40,48},{48,56},{56,0},{1,9},... | collective-permute-start | bytes 3145736 | tf_op jit(solution)/shard_map/ppermute | solution.py:367
  41.5 24.1 %collective-permute-start.4 = (bf16[8,512,128]{2,1,0:T(8,128)(2,1)S(1)}, bf16[8,512,128]{2,1,0:T(8,128)(2,1)S(1)}, u32[]{:S(2)}, u32[]{:S(2)}) collective-permute-start(bf16[8,512,128]{2,1,0:T(8,128)(2,1)S(1)} %all-to-all-done.refs_0_), channel_id=1, source_target_pairs={{0,6},{2,0},{4,2},{6,4},{1,7},{3,1},{5,3},{7,5},{8,14},{10,8},{12,... | collective-permute-start | bytes 3145736 | tf_op jit(solution)/shard_map/ppermute | solution.py:367
  44.1 25.0 %collective-permute-start.1 = (bf16[8,512,128]{2,1,0:T(8,128)(2,1)S(1)}, bf16[8,512,128]{2,1,0:T(8,128)(2,1)S(1)}, u32[]{:S(2)}, u32[]{:S(2)}) collective-permute-start(bf16[8,512,128]{2,1,0:T(8,128)(2,1)S(1)} %all-to-all-done.refs_0_), channel_id=1, source_target_pairs={{0,2},{2,4},{4,6},{6,0},{1,3},{3,5},{5,7},{7,1},{8,10},{10,12},{12... | collective-permute-start | bytes 3145736 | tf_op jit(solution)/shard_map/ppermute | solution.py:367
  59.1 24.6 %collective-permute-start.16 = (bf16[16,128,256]{2,1,0:T(8,128)(2,1)S(1)}, bf16[16,128,256]{2,1,0:T(8,128)(2,1)S(1)}, u32[]{:S(2)}, u32[]{:S(2)}) collective-permute-start(bf16[16,128,256]{2,1,0:T(8,128)(2,1)S(1)} %collective-permute-done.14.refs_12_), channel_id=1, source_target_pairs={{0,56},{8,0},{16,8},{24,16},{32,24},{40,32},{48,40},{56,48},{1,57}... | collective-permute-start | bytes 3145736 | tf_op jit(solution)/shard_map/ppermute | solution.py:367
  62.3 26.8 %collective-permute-start.15 = (bf16[16,128,256]{2,1,0:T(8,128)(2,1)}, bf16[16,128,256]{2,1,0:T(8,128)(2,1)S(1)}, u32[]{:S(2)}, u32[]{:S(2)}) collective-permute-start(bf16[16,128,256]{2,1,0:T(8,128)(2,1)} %collective-permute-done.13.refs_11_), channel_id=1, source_target_pairs={{0,8},{8,16},{16,24},{24,32},{32,40},{40,48},{48,56},{56,0},{1,9},... | collective-permute-start | bytes 3145736 | tf_op jit(solution)/shard_map/ppermute | solution.py:367
  65.6 23.8 %collective-permute-start.5 = (bf16[8,256,128]{2,1,0:T(8,128)(2,1)S(1)}, bf16[8,256,128]{2,1,0:T(8,128)(2,1)S(1)}, u32[]{:S(2)}, u32[]{:S(2)}) collective-permute-start(bf16[8,256,128]{2,1,0:T(8,128)(2,1)S(1)} %slice.21), channel_id=1, source_target_pairs={{0,6},{2,0},{4,2},{6,4},{1,7},{3,1},{5,3},{7,5},{8,14},{10,8},{12,... | collective-permute-start | bytes 1572872 | tf_op jit(solution)/shard_map/ppermute | solution.py:367
  69.2 20.2 %collective-permute-start.3 = (bf16[8,256,128]{2,1,0:T(8,128)(2,1)S(1)}, bf16[8,256,128]{2,1,0:T(8,128)(2,1)S(1)}, u32[]{:S(2)}, u32[]{:S(2)}) collective-permute-start(bf16[8,256,128]{2,1,0:T(8,128)(2,1)S(1)} %slice.20), channel_id=1, source_target_pairs={{0,2},{2,4},{4,6},{6,0},{1,3},{3,5},{5,7},{7,1},{8,10},{10,12},{12... | collective-permute-start | bytes 1572872 | tf_op jit(solution)/shard_map/ppermute | solution.py:367
  83.7 6.1 %collective-permute-start.8 = (bf16[8,512,128]{2,1,0:T(8,128)(2,1)S(1)}, bf16[8,512,128]{2,1,0:T(8,128)(2,1)S(1)}, u32[]{:S(2)}, u32[]{:S(2)}) collective-permute-start(bf16[8,512,128]{2,1,0:T(8,128)(2,1)S(1)} %collective-permute-done.4.refs_8_), channel_id=1, source_target_pairs={{0,1},{1,0},{2,3},{3,2},{4,5},{5,4},{6,7},{7,6},{8,9},{9,8},{10,11... | collective-permute-start | bytes 3145736 | tf_op jit(solution)/shard_map/ppermute | solution.py:367
  85.7 26.0 %collective-permute-start.18 = (bf16[16,128,256]{2,1,0:T(8,128)(2,1)S(1)}, bf16[16,128,256]{2,1,0:T(8,128)(2,1)S(1)}, u32[]{:S(2)}, u32[]{:S(2)}) collective-permute-start(bf16[16,128,256]{2,1,0:T(8,128)(2,1)S(1)} %collective-permute-done.16.refs_14_), channel_id=1, source_target_pairs={{0,56},{8,0},{16,8},{24,16},{32,24},{40,32},{48,40},{56,48},{1,57}... | collective-permute-start | bytes 3145736 | tf_op jit(solution)/shard_map/ppermute | solution.py:367
  89.1 23.4 %collective-permute-start.2 = (bf16[8,512,128]{2,1,0:T(8,128)(2,1)S(1)}, bf16[8,512,128]{2,1,0:T(8,128)(2,1)S(1)}, u32[]{:S(2)}, u32[]{:S(2)}) collective-permute-start(bf16[8,512,128]{2,1,0:T(8,128)(2,1)S(1)} %collective-permute-done.1.refs_2_), channel_id=1, source_target_pairs={{0,1},{1,0},{2,3},{3,2},{4,5},{5,4},{6,7},{7,6},{8,9},{9,8},{10,11... | collective-permute-start | bytes 3145736 | tf_op jit(solution)/shard_map/ppermute | solution.py:367
  89.4 26.6 %collective-permute-start.17 = (bf16[16,128,256]{2,1,0:T(8,128)(2,1)S(1)}, bf16[16,128,256]{2,1,0:T(8,128)(2,1)S(1)}, u32[]{:S(2)}, u32[]{:S(2)}) collective-permute-start(bf16[16,128,256]{2,1,0:T(8,128)(2,1)S(1)} %collective-permute-done.15.refs_13_), channel_id=1, source_target_pairs={{0,8},{8,16},{16,24},{24,32},{32,40},{40,48},{48,56},{56,0},{1,9},... | collective-permute-start | bytes 3145736 | tf_op jit(solution)/shard_map/ppermute | solution.py:367
  89.4 26.7 %collective-permute-start = (bf16[8,512,128]{2,1,0:T(8,128)(2,1)S(1)}, bf16[8,512,128]{2,1,0:T(8,128)(2,1)S(1)}, u32[]{:S(2)}, u32[]{:S(2)}) collective-permute-start(bf16[8,512,128]{2,1,0:T(8,128)(2,1)S(1)} %all-to-all-done.refs_0_), channel_id=1, source_target_pairs={{0,1},{1,0},{2,3},{3,2},{4,5},{5,4},{6,7},{7,6},{8,9},{9,8},{10,11... | collective-permute-start | bytes 3145736 | tf_op jit(solution)/shard_map/ppermute | solution.py:367
  89.8 26.4 %collective-permute-start.7 = (bf16[8,256,128]{2,1,0:T(8,128)(2,1)S(1)}, bf16[8,256,128]{2,1,0:T(8,128)(2,1)S(1)}, u32[]{:S(2)}, u32[]{:S(2)}) collective-permute-start(bf16[8,256,128]{2,1,0:T(8,128)(2,1)S(1)} %collective-permute-done.5.refs_5_), channel_id=1, source_target_pairs={{0,1},{1,0},{2,3},{3,2},{4,5},{5,4},{6,7},{7,6},{8,9},{9,8},{10,11... | collective-permute-start | bytes 1572872 | tf_op jit(solution)/shard_map/ppermute | solution.py:367
  111.7 4.5 %collective-permute-start.6 = (bf16[8,256,128]{2,1,0:T(8,128)(2,1)S(1)}, bf16[8,256,128]{2,1,0:T(8,128)(2,1)S(1)}, u32[]{:S(2)}, u32[]{:S(2)}) collective-permute-start(bf16[8,256,128]{2,1,0:T(8,128)(2,1)S(1)} %collective-permute-done.3.refs_4_), channel_id=1, source_target_pairs={{0,1},{1,0},{2,3},{3,2},{4,5},{5,4},{6,7},{7,6},{8,9},{9,8},{10,11... | collective-permute-start | bytes 1572872 | tf_op jit(solution)/shard_map/ppermute | solution.py:367
  112.5 16.7 %collective-permute-start.20 = (bf16[9,128,256]{2,1,0:T(8,128)(2,1)S(1)}, bf16[9,128,256]{2,1,0:T(8,128)(2,1)S(1)}, u32[]{:S(2)}, u32[]{:S(2)}) collective-permute-start(bf16[9,128,256]{2,1,0:T(8,128)(2,1)S(1)} %slice.23), channel_id=1, source_target_pairs={{0,56},{8,0},{16,8},{24,16},{32,24},{40,32},{48,40},{56,48},{1,57}... | collective-permute-start | bytes 1769480 | tf_op jit(solution)/shard_map/ppermute | solution.py:367
  116.1 13.1 %collective-permute-start.19 = (bf16[7,128,256]{2,1,0:T(8,128)(2,1)S(1)}, bf16[7,128,256]{2,1,0:T(8,128)(2,1)S(1)}, u32[]{:S(2)}, u32[]{:S(2)}) collective-permute-start(bf16[7,128,256]{2,1,0:T(8,128)(2,1)S(1)} %slice.22), channel_id=1, source_target_pairs={{0,8},{8,16},{16,24},{24,32},{32,40},{40,48},{48,56},{56,0},{1,9},... | collective-permute-start | bytes 1376264 | tf_op jit(solution)/shard_map/ppermute | solution.py:367
  159.0 8.8 %collective-permute-start.21 = (f32[128,512]{1,0:T(8,128)S(1)}, f32[128,512]{1,0:T(8,128)S(1)}, u32[]{:S(2)}, u32[]{:S(2)}) collective-permute-start(f32[128,512]{1,0:T(8,128)S(1)} %get-tuple-element.39), channel_id=1, source_target_pairs={{0,128},{64,192},{128,0},{192,64},{1,129},{65,193},{129,1},{193,65... | collective-permute-start | bytes 786440 | tf_op jit(solution)/shard_map/ppermute | solution.py:367
  161.2 13.3 %collective-permute-start.22 = (f32[128,512]{1,0:T(8,128)S(1)}, f32[128,512]{1,0:T(8,128)S(1)}, u32[]{:S(2)}, u32[]{:S(2)}) collective-permute-start(f32[128,512]{1,0:T(8,128)S(1)} %get-tuple-element.40), channel_id=1, source_target_pairs={{0,64},{64,128},{128,192},{192,0},{1,65},{65,129},{129,193},{193,1... | collective-permute-start | bytes 786440 | tf_op jit(solution)/shard_map/ppermute | solution.py:367
  161.9 12.6 %collective-permute-start.23 = (f32[128,512]{1,0:T(8,128)S(1)}, f32[128,512]{1,0:T(8,128)S(1)}, u32[]{:S(2)}, u32[]{:S(2)}) collective-permute-start(f32[128,512]{1,0:T(8,128)S(1)} %get-tuple-element.41), channel_id=1, source_target_pairs={{0,192},{64,0},{128,64},{192,128},{1,193},{65,1},{129,65},{193,129... | collective-permute-start | bytes 786440 | tf_op jit(solution)/shard_map/ppermute | solution.py:367
  (17 other events, 469.9 us)
